TPU v7x, 128 devices: a whole 4x4x4 slice. The times are simulated.
128 devices in a mesh: section: 2 (over core), shard: 8 (over y_lo, x), context: 4 (over z), tensor: 2 (over y_hi).
Axes of the slice: x: 4, y: 4 (y_hi: 2, y_lo: 2; y = y_hi * 2 + y_lo), z: 4, core: 2. Of those that a mesh axis runs over, the one named last changes fastest.
Arguments:
- block_input: bfloat16 [2, 8, 1024, 768], P(None, 'shard', ('context', 'tensor')), may hold values from -36 to 36
- cotangent: bfloat16 [2, 8, 1024, 768], P(None, 'shard', ('context', 'tensor')), may hold values from -6 to 6
- segment_ids: int32 [2, 8, 1024], P(None, 'shard'), may hold values from 0 to 7, as said below
- w_qkv: bfloat16 [2, 768, 2304], P('section', 'shard'), may hold values from -0.21875 to 0.21875
- w_out: bfloat16 [2, 768, 768], P('section', 'shard'), may hold values from -1.75 to 1.75
- w_fc: bfloat16 [2, 768, 3072], P('section', 'shard', 'tensor'), may hold values from -0.21875 to 0.21875
- w_proj: bfloat16 [2, 3072, 768], P('section', 'tensor', 'shard'), may hold values from -0.109375 to 0.109375
- norm_gains: bfloat16 [2, 2, 768], P('section', None, 'shard'), may hold values from 0.25 to 1.75
- norm_biases: bfloat16 [2, 2, 768], P('section', None, 'shard'), may hold values from -3 to 3
Outputs:
- block_outputs: bfloat16 [2, 2, 8, 1024, 768], P('section', None, 'shard', ('context', 'tensor'))
- input_grads: bfloat16 [2, 2, 8, 1024, 768], P('section', None, 'shard', ('context', 'tensor'))
- grad_qkv: float32 [2, 768, 2304], P('section', 'shard')
- grad_out: float32 [2, 768, 768], P('section', 'shard')
- grad_fc: float32 [2, 768, 3072], P('section', 'shard', 'tensor')
- grad_proj: float32 [2, 3072, 768], P('section', 'tensor', 'shard')
- grad_gains: float32 [2, 2, 768], P('section', None, 'shard')
- grad_bias_attention: float32 [2, 768], P('section', 'shard')
- grad_bias_feedforward: float32 [2, 768], P('section', 'shard')
Inputs may be any that keep to these rules, and one draw needn't show every extreme that they name: `segment_ids`: along each sequence the ids start at 0 and never fall; in each group of 2 sequences of one index of the second dimension, one sequence drawn from the seed is a single document.
All inputs are finite; a program needn't handle non-finite values.
Results may differ from a plain program's by a relative error of at most 0.03.
Values may be sent and summed in bfloat16 or wider, within the bound.
A program may use at most 192 MiB of HBM per device.

v0:
```python
import math

import jax
import jax.numpy as jnp
from jax import lax
from jax.sharding import PartitionSpec as P

HEAD_DIM = 64


EPSILON = 1e-05
MASKED = -1000000000.0


def passed_along(block, axis, distance):
    devices = range(lax.axis_size(axis))
    route = [(i - distance, i) for i in devices if i - distance in devices]
    return lax.ppermute(block, axis, route)


def layer_norm(values, gain_vec, bias_vec):
    row_mean = jnp.mean(values, -1, keepdims=True)
    centred = values - row_mean
    variance = jnp.mean(centred * centred, -1, keepdims=True)
    return centred * lax.rsqrt(variance + EPSILON) * gain_vec + bias_vec


def smooth_unit(values):
    return jax.nn.gelu(values, approximate=True)


def transpose_product(first_op, second_op):
    return lax.dot_general(
        first_op, second_op, (((0,), (0,)), ((), ())), preferred_element_type=jnp.float32
    )


def product_transposed(first_op, second_op):
    return lax.dot_general(
        first_op, second_op, (((1,), (1,)), ((), ())), preferred_element_type=jnp.float32
    )


def flatten_rows(stacked):
    return stacked.reshape(-1, stacked.shape[-1])


def unpack(fetched):
    return tuple((member[0] for member in fetched))


def per_device(
    block_input, cotangent, segment_ids, w_qkv, w_out, w_fc, w_proj, norm_gains, norm_biases
):
    section_index = lax.axis_index("section")
    micro_count = block_input.shape[0]
    tok_rows = block_input.shape[2]
    feat_width = block_input.shape[3]
    seq_length = segment_ids.shape[2]
    head_count = feat_width // HEAD_DIM
    score_scale = 1.0 / math.sqrt(HEAD_DIM)
    span_index = lax.axis_index("context") * lax.axis_size("tensor") + lax.axis_index("tensor")
    query_pos = span_index * tok_rows + jnp.arange(tok_rows)
    key_pos = jnp.arange(seq_length)
    causal = key_pos[None, :] <= query_pos[:, None]
    blank_rows = jnp.zeros((1, tok_rows, feat_width), jnp.bfloat16)
    empty_rows = jnp.zeros((tok_rows, feat_width), jnp.bfloat16)
    step_ids = jnp.arange(micro_count + 1)
    weight_set = unpack(
        (
            lax.all_gather(w_qkv, "shard", axis=1, tiled=True),
            lax.all_gather(w_out, "shard", axis=1, tiled=True),
            lax.all_gather(w_fc, "shard", axis=1, tiled=True),
            lax.all_gather(w_proj, "shard", axis=2, tiled=True),
            lax.all_gather(norm_gains, "shard", axis=2, tiled=True),
            lax.all_gather(norm_biases, "shard", axis=2, tiled=True),
        )
    )

    def split_heads(matrix):
        return matrix.reshape(matrix.shape[0], head_count, HEAD_DIM)

    def attend_mask(micro_index):
        seg_row = segment_ids[micro_index, 0]
        seg_query = lax.dynamic_slice_in_dim(seg_row, span_index * tok_rows, tok_rows, 0)
        return causal & (seg_row[None, :] == seg_query[:, None])

    def masked_scores(query, keys, allowed):
        raw_scores = jnp.einsum(
            "qhd,khd->hqk",
            split_heads(query),
            split_heads(keys),
            preferred_element_type=jnp.float32,
        )
        return jnp.where(allowed[None], raw_scores * score_scale, MASKED)

    inputs_pad = jnp.concatenate([block_input[:, 0], blank_rows], 0)

    def forward_step(received, step):
        qkv_full, out_full, fc_full, proj_full, gain_full, bias_full = weight_set
        gain_float = gain_full.astype(jnp.float32)
        bias_float = bias_full.astype(jnp.float32)
        micro_index = jnp.clip(step - section_index, 0, micro_count - 1)
        entry = jnp.where(section_index == 0, inputs_pad[step], received)
        inputs = entry.astype(jnp.float32)
        normed = layer_norm(inputs, gain_float[0], bias_float[0]).astype(jnp.bfloat16)
        projected = jnp.dot(normed, qkv_full, preferred_element_type=jnp.float32).astype(
            jnp.bfloat16
        )
        query = projected[:, :feat_width]
        keys, values = (
            lax.all_gather(
                projected[:, feat_width : 2 * feat_width], ("context", "tensor"), axis=0, tiled=True
            ),
            lax.all_gather(
                projected[:, 2 * feat_width :], ("context", "tensor"), axis=0, tiled=True
            ),
        )
        masked = masked_scores(query, keys, attend_mask(micro_index))
        totals = jax.nn.logsumexp(masked, axis=-1)
        probs_low = jnp.exp(masked - totals[..., None]).astype(jnp.bfloat16)
        mixed = jnp.einsum(
            "hqk,khd->qhd", probs_low, split_heads(values), preferred_element_type=jnp.float32
        )
        mixed = mixed.reshape(tok_rows, feat_width).astype(jnp.bfloat16)
        resid = inputs + jnp.dot(mixed, out_full, preferred_element_type=jnp.float32)
        inner = layer_norm(resid, gain_float[1], bias_float[1]).astype(jnp.bfloat16)
        inner_all = lax.all_gather(inner, "tensor", axis=0, tiled=True)
        upward = jnp.dot(inner_all, fc_full, preferred_element_type=jnp.float32)
        active = smooth_unit(upward).astype(jnp.bfloat16)
        downward = lax.psum_scatter(
            jnp.dot(active, proj_full, preferred_element_type=jnp.float32).astype(jnp.bfloat16),
            "tensor",
            scatter_dimension=0,
            tiled=True,
        ).astype(jnp.float32)
        sent = (resid + downward).astype(jnp.bfloat16)
        passed = passed_along(sent, "section", 1)
        return (
            passed,
            (
                sent,
                entry,
                normed,
                query,
                keys,
                values,
                totals,
                mixed,
                resid,
                inner_all,
                upward,
                active,
            ),
        )

    _, fwd_kept = lax.scan(forward_step, empty_rows, step_ids)
    fwd_kept = jax.tree.map(
        lambda stacked: lax.dynamic_slice_in_dim(stacked, section_index, micro_count, 0), fwd_kept
    )
    weight_set = unpack(
        (
            lax.all_gather(w_qkv, "shard", axis=1, tiled=True),
            lax.all_gather(w_out, "shard", axis=1, tiled=True),
            lax.all_gather(w_fc, "shard", axis=1, tiled=True),
            lax.all_gather(w_proj, "shard", axis=2, tiled=True),
            lax.all_gather(norm_gains, "shard", axis=2, tiled=True),
            lax.all_gather(norm_biases, "shard", axis=2, tiled=True),
        )
    )
    grads_pad = jnp.concatenate([cotangent[:, 0], blank_rows], 0)

    def backward_step(received, step):
        qkv_full, out_full, fc_full, proj_full, gain_full, bias_full = weight_set
        gain_float = gain_full.astype(jnp.float32)
        bias_float = bias_full.astype(jnp.float32)
        micro_index = jnp.clip(step - 1 + section_index, 0, micro_count - 1)
        saved = jax.tree.map(lambda stacked: stacked[micro_index], fwd_kept)
        entry = saved[1]
        query = saved[3]
        keys = saved[4]
        values = saved[5]
        totals = saved[6]
        resid = saved[8]
        upward = saved[10]
        incoming = jnp.where(section_index == 1, grads_pad[step], received)
        outer_grad = incoming.astype(jnp.float32)
        incoming_all = lax.all_gather(incoming, "tensor", axis=0, tiled=True)
        active_grad = product_transposed(incoming_all, proj_full)
        _, unit_pull = jax.vjp(smooth_unit, upward)
        upward_grad = unit_pull(active_grad)[0].astype(jnp.bfloat16)
        inner_grad = lax.psum_scatter(
            product_transposed(upward_grad, fc_full).astype(jnp.bfloat16),
            "tensor",
            scatter_dimension=0,
            tiled=True,
        ).astype(jnp.float32)
        _, late_pull = jax.vjp(layer_norm, resid, gain_float[1], bias_float[1])
        resid_part, gain_late, bias_late = late_pull(inner_grad)
        resid_grad = outer_grad + resid_part
        resid_low = resid_grad.astype(jnp.bfloat16)
        mixed_grad = product_transposed(resid_low, out_full).astype(jnp.bfloat16)
        masked = masked_scores(query, keys, attend_mask(micro_index))
        probs = jnp.exp(masked - totals[..., None])
        probs_low = probs.astype(jnp.bfloat16)
        mixed_heads = split_heads(mixed_grad)
        query_heads = split_heads(query)
        prob_grad = jnp.einsum(
            "qhd,khd->hqk", mixed_heads, split_heads(values), preferred_element_type=jnp.float32
        )
        centre = jnp.sum(probs * prob_grad, -1, keepdims=True)
        score_grad = (probs * (prob_grad - centre)).astype(jnp.bfloat16)
        query_grad = (
            jnp.einsum(
                "hqk,khd->qhd", score_grad, split_heads(keys), preferred_element_type=jnp.float32
            )
            * score_scale
        )
        key_part = (
            jnp.einsum("hqk,qhd->khd", score_grad, query_heads, preferred_element_type=jnp.float32)
            * score_scale
        )
        value_part = jnp.einsum(
            "hqk,qhd->khd", probs_low, mixed_heads, preferred_element_type=jnp.float32
        )
        pair_grad = lax.psum_scatter(
            jnp.concatenate(
                [
                    key_part.reshape(tok_rows * lax.axis_size(("context", "tensor")), feat_width),
                    value_part.reshape(tok_rows * lax.axis_size(("context", "tensor")), feat_width),
                ],
                1,
            ).astype(jnp.bfloat16),
            ("context", "tensor"),
            scatter_dimension=0,
            tiled=True,
        ).astype(jnp.float32)
        projected_grad = jnp.concatenate(
            [query_grad.reshape(tok_rows, feat_width), pair_grad], 1
        ).astype(jnp.bfloat16)
        normed_grad = product_transposed(projected_grad, qkv_full)
        _, early_pull = jax.vjp(layer_norm, entry.astype(jnp.float32), gain_float[0], bias_float[0])
        input_part, gain_early, bias_early = early_pull(normed_grad)
        sent_grad = (resid_grad + input_part).astype(jnp.bfloat16)
        passed = passed_along(sent_grad, "section", -1)
        gain_terms = jnp.stack([gain_early, gain_late])
        bias_terms = jnp.stack([bias_early, bias_late])
        return (
            passed,
            (
                sent_grad,
                projected_grad,
                resid_low,
                incoming_all,
                upward_grad,
                gain_terms,
                bias_terms,
            ),
        )

    _, bwd_kept = lax.scan(backward_step, empty_rows, step_ids)
    bwd_kept = jax.tree.map(
        lambda stacked: lax.dynamic_slice_in_dim(stacked, 1 - section_index, micro_count, 0),
        bwd_kept,
    )
    sent_grads, projected_grads, resid_lows, incoming_alls, upward_grads, gain_terms, bias_terms = (
        bwd_kept
    )
    sent_outs = fwd_kept[0]
    normed_kept = fwd_kept[2]
    mixed_kept = fwd_kept[7]
    inner_kept = fwd_kept[9]
    active_kept = fwd_kept[11]
    qkv_grad = transpose_product(flatten_rows(normed_kept), flatten_rows(projected_grads))
    out_grad = transpose_product(flatten_rows(mixed_kept), flatten_rows(resid_lows))
    fc_grad = transpose_product(flatten_rows(inner_kept), flatten_rows(upward_grads))
    proj_grad = transpose_product(flatten_rows(active_kept), flatten_rows(incoming_alls))
    gain_grad = jnp.sum(gain_terms, 0)
    bias_grad = jnp.sum(bias_terms, 0)
    qkv_part, out_part, gain_part, bias_part = (
        lax.psum_scatter(qkv_grad, ("shard", "context", "tensor"), scatter_dimension=0, tiled=True),
        lax.psum_scatter(out_grad, ("shard", "context", "tensor"), scatter_dimension=0, tiled=True),
        lax.psum_scatter(
            gain_grad, ("shard", "context", "tensor"), scatter_dimension=1, tiled=True
        ),
        lax.psum_scatter(
            bias_grad, ("shard", "context", "tensor"), scatter_dimension=1, tiled=True
        ),
    )
    qkv_part, out_part, gain_part, bias_part = (
        lax.all_gather(
            qkv_part.astype(jnp.bfloat16), ("context", "tensor"), axis=0, tiled=True
        ).astype(qkv_part.dtype),
        lax.all_gather(
            out_part.astype(jnp.bfloat16), ("context", "tensor"), axis=0, tiled=True
        ).astype(out_part.dtype),
        lax.all_gather(
            gain_part.astype(jnp.bfloat16), ("context", "tensor"), axis=1, tiled=True
        ).astype(gain_part.dtype),
        lax.all_gather(
            bias_part.astype(jnp.bfloat16), ("context", "tensor"), axis=1, tiled=True
        ).astype(bias_part.dtype),
    )
    fc_part, proj_part = (
        lax.psum_scatter(
            fc_grad.astype(jnp.bfloat16), ("shard", "context"), scatter_dimension=0, tiled=True
        ).astype(jnp.float32),
        lax.psum_scatter(
            proj_grad.astype(jnp.bfloat16), ("shard", "context"), scatter_dimension=1, tiled=True
        ).astype(jnp.float32),
    )
    fc_part, proj_part = (
        lax.all_gather(fc_part.astype(jnp.bfloat16), "context", axis=0, tiled=True).astype(
            fc_part.dtype
        ),
        lax.all_gather(proj_part.astype(jnp.bfloat16), "context", axis=1, tiled=True).astype(
            proj_part.dtype
        ),
    )
    block_outputs = sent_outs[None, :, None]
    input_grads = sent_grads[None, :, None]
    return (
        block_outputs,
        input_grads,
        qkv_part[None],
        out_part[None],
        fc_part[None],
        proj_part[None],
        gain_part[None],
        bias_part[None, 0],
        bias_part[None, 1],
    )


def solution(mesh):
    in_specs = (
        P(None, "shard", ("context", "tensor"), None),
        P(None, "shard", ("context", "tensor"), None),
        P(None, "shard", None),
        P("section", "shard", None),
        P("section", "shard", None),
        P("section", "shard", "tensor"),
        P("section", "tensor", "shard"),
        P("section", None, "shard"),
        P("section", None, "shard"),
    )
    out_specs = (
        P("section", None, "shard", ("context", "tensor"), None),
        P("section", None, "shard", ("context", "tensor"), None),
        P("section", "shard", None),
        P("section", "shard", None),
        P("section", "shard", "tensor"),
        P("section", "tensor", "shard"),
        P("section", None, "shard"),
        P("section", "shard"),
        P("section", "shard"),
    )
    return jax.shard_map(
        per_device, mesh=mesh, in_specs=in_specs, out_specs=out_specs, check_vma=False
    )
```

profile of v0, /device:TPU:0, one launch (start us, length us, event | category | flops | bytes accessed | tf_op | source)
XLA Modules:
  0.0 2026.2 jit_solution(14851975570762218590)
XLA Ops:
  10.9 29.7 %all_gather.69 = bf16[1,2,768]{1,0,2:T(2,128)(2,1)S(1)} all-gather(bf16[1,2,96]{1,0,2:T(2,128)(2,1)S(1)} %copy.92), channel_id=1, replica_groups=mesh['section'=2,'shard'=8,'context'=4,'tensor'=2] {'shard'}, dimensions={2}, use_global_device_ids=true | all-gather | bytes 3456 | tf_op jit(solution)/shard_map/all_gather | solution.py:75
  41.7 29.3 %all_gather.70 = bf16[1,2,768]{1,0,2:T(2,128)(2,1)S(1)} all-gather(bf16[1,2,96]{1,0,2:T(2,128)(2,1)S(1)} %copy.94), channel_id=1, replica_groups=mesh['section'=2,'shard'=8,'context'=4,'tensor'=2] {'shard'}, dimensions={2}, use_global_device_ids=true | all-gather | bytes 3456 | tf_op jit(solution)/shard_map/all_gather | solution.py:76
  77.9 18.0 all-gather.13.cloned.1.call-done
  95.8 42.8 %all-gather.15.cloned.1.call-done = bf16[1,768,1536]{2,1,0:T(8,128)(2,1)} async-done(((bf16[1,96,1536]{2,1,0:T(8,128)(2,1)}), bf16[1,768,1536]{2,1,0:T(8,128)(2,1)}) %all-gather.15.cloned.1.call-update) | async-done | bytes 2359312 | tf_op jit(solution)/shard_map/all_gather | solution.py:73
  138.6 46.8 %all-gather.11.cloned.1.call-done = bf16[1,768,2304]{2,1,0:T(8,128)(2,1)} async-done(((bf16[1,96,2304]{2,1,0:T(8,128)(2,1)}), bf16[1,768,2304]{2,1,0:T(8,128)(2,1)}) %all-gather.11.cloned.1.call-update) | async-done | bytes 3538960 | tf_op jit(solution)/shard_map/all_gather | solution.py:71
  189.8 446.9 %while.66 = (s32[]{:T(128)}, bf16[128,768]{1,0:T(8,128)(2,1)S(1)}, bf16[3,128,768]{2,1,0:T(8,128)(2,1)}, bf16[3,128,768]{2,1,0:T(8,128)(2,1)}, bf16[3,128,768]{1...) while((s32[]{:T(128)}, bf16[128,768]{1,0:T(8,128)(2,1)S(1)}, ...), condition=%wide.region_8.9_spmd.clone, body=%wide.region_0.8_spmd.clone.sunk | while | flops 2243214592 | bytes 153501280 | solution.py:157
  203.1 44.3 %all-gather.21.cloned.1.call-done = bf16[1024,768]{1,0:T(8,128)(2,1)} async-done(((bf16[128,768]{1,0:T(8,128)(2,1)}), bf16[1024,768]{1,0:T(8,128)(2,1)}) %all-gather.21.cloned.1.call-update) | async-done | bytes 1572880 | tf_op jit(solution)/shard_map/while/body/eval_jaxpr/all_gather | solution.py:112
  253.1 45.4 %all-gather.19.cloned.1.call-done = bf16[1024,768]{1,0:T(8,128)(2,1)} async-done(((bf16[128,768]{1,0:T(8,128)(2,1)}), bf16[1024,768]{1,0:T(8,128)(2,1)}) %all-gather.19.cloned.1.call-update) | async-done | bytes 1572880 | tf_op jit(solution)/shard_map/while/body/eval_jaxpr/all_gather | solution.py:115
  300.2 4.4 fusion.197
  305.5 8.4 all_gather.91
  352.2 44.1 %all-gather.21.cloned.1.call-done = bf16[1024,768]{1,0:T(8,128)(2,1)} async-done(((bf16[128,768]{1,0:T(8,128)(2,1)}), bf16[1024,768]{1,0:T(8,128)(2,1)}) %all-gather.21.cloned.1.call-update) | async-done | bytes 1572880 | tf_op jit(solution)/shard_map/while/body/eval_jaxpr/all_gather | solution.py:112
  402.0 45.5 %all-gather.19.cloned.1.call-done = bf16[1024,768]{1,0:T(8,128)(2,1)} async-done(((bf16[128,768]{1,0:T(8,128)(2,1)}), bf16[1024,768]{1,0:T(8,128)(2,1)}) %all-gather.19.cloned.1.call-update) | async-done | bytes 1572880 | tf_op jit(solution)/shard_map/while/body/eval_jaxpr/all_gather | solution.py:115
  449.3 4.4 fusion.197
  454.5 8.4 all_gather.91
  501.1 44.3 %all-gather.21.cloned.1.call-done = bf16[1024,768]{1,0:T(8,128)(2,1)} async-done(((bf16[128,768]{1,0:T(8,128)(2,1)}), bf16[1024,768]{1,0:T(8,128)(2,1)}) %all-gather.21.cloned.1.call-update) | async-done | bytes 1572880 | tf_op jit(solution)/shard_map/while/body/eval_jaxpr/all_gather | solution.py:112
  551.1 45.4 %all-gather.19.cloned.1.call-done = bf16[1024,768]{1,0:T(8,128)(2,1)} async-done(((bf16[128,768]{1,0:T(8,128)(2,1)}), bf16[1024,768]{1,0:T(8,128)(2,1)}) %all-gather.19.cloned.1.call-update) | async-done | bytes 1572880 | tf_op jit(solution)/shard_map/while/body/eval_jaxpr/all_gather | solution.py:115
  598.2 4.4 fusion.197
  603.4 8.4 all_gather.91
  655.0 440.9 %while.67 = (s32[]{:T(128)}, bf16[128,768]{1,0:T(8,128)(2,1)S(1)}, bf16[3,128,768]{2,1,0:T(8,128)(2,1)}, bf16[3,128,2304]{2,1,0:T(8,128)(2,1)}, bf16[3,128,768]{...) while((s32[]{:T(128)}, bf16[128,768]{1,0:T(8,128)(2,1)S(1)}, ...), condition=%wide.region_25.26_spmd.clone, body=%wide.region_9.25_spmd.clone.sunk | while | flops 2867824384 | bytes 222465904 | solution.py:261
  659.6 9.4 all_gather.92
  669.6 4.6 bitcast_dynamic-update-slice_fusion.21
  687.6 4.9 reduce-scatter.22.cloned.1.call-done
  699.6 4.8 fusion.224
  722.3 70.4 %reduce-scatter.24.cloned.1.call-done = bf16[128,1536]{1,0:T(8,128)(2,1)} async-done(((bf16[1024,1536]{1,0:T(8,128)(2,1)}), bf16[128,1536]{1,0:T(8,128)(2,1)}) %reduce-scatter.24.cloned.1.call-update) | async-done | bytes 393232 | tf_op jit(solution)/shard_map/while
  806.7 9.6 all_gather.92
  817.0 4.6 bitcast_dynamic-update-slice_fusion.21
  846.3 4.8 fusion.224
  869.0 70.4 %reduce-scatter.24.cloned.1.call-done = bf16[128,1536]{1,0:T(8,128)(2,1)} async-done(((bf16[1024,1536]{1,0:T(8,128)(2,1)}), bf16[128,1536]{1,0:T(8,128)(2,1)}) %reduce-scatter.24.cloned.1.call-update) | async-done | bytes 393232 | tf_op jit(solution)/shard_map/while
  953.3 9.6 all_gather.92
  963.6 4.6 bitcast_dynamic-update-slice_fusion.21
  993.0 4.8 fusion.224
  1015.7 70.3 %reduce-scatter.24.cloned.1.call-done = bf16[128,1536]{1,0:T(8,128)(2,1)} async-done(((bf16[1024,1536]{1,0:T(8,128)(2,1)}), bf16[128,1536]{1,0:T(8,128)(2,1)}) %reduce-scatter.24.cloned.1.call-update) | async-done | bytes 393232 | tf_op jit(solution)/shard_map/while
  1095.9 4.6 bitcast_convert_fusion
  1112.4 297.4 %fusion.98 = (f32[16,2304]{1,0:T(8,128)S(1)}, f32[16,768]{1,0:T(8,128)S(1)}) fusion(f32[768,2304]{1,0:T(8,128)} %convolution_bitcast_fusion, f32[768,768]{1,0:T(8,128)S(1)} %convolution_bitcast_fusion.1), kind=kCustom, calls=%all-reduce-scatter.2 | all-reduce-scatter fusion | flops 3145729 | bytes 9634304
  1409.9 6.9 collective-permute-start.18
  1416.8 12.3 collective-permute-start.19
  1429.1 15.2 collective-permute-start.20
  1447.3 7.1 collective-permute-start.33
  1454.6 341.6 %all-reduce.8 = (bf16[2,768]{1,0:T(2,128)(2,1)S(1)}, bf16[2,768]{1,0:T(2,128)(2,1)S(1)}) all-reduce(f32[2,768]{1,0:T(2,128)S(1)} %dynamic-slice_reduce_fusion.2, f32[2,768]{1,0:T(2,128)S(1)} %dynamic-slice_reduce_fusion.1), channel_id=9, replica_groups=mesh['section'=2,'shard'=8,'context'=4,'tensor'=2] {'shard','context','t..., use_global_device_ids=true, to_apply=%region_31.32.clone | all-reduce | flops 3072 | bytes 18432
  1796.3 18.0 all-gather.3
  1819.9 20.4 %all-gather.2 = bf16[8,12,2]{1,2,0:T(2,128)(2,1)S(1)} all-gather(bf16[1,12,2]{1,2,0:T(2,128)(2,1)S(1)} %fusion.96), channel_id=1, replica_groups=mesh['section'=2,'shard'=8,'context'=4,'tensor'=2] {'context','tensor'}, dimensions={0}, use_global_device_ids=true | all-gather | bytes 432 | tf_op jit(solution)/shard_map/all_gather | solution.py:297
  1847.3 10.0 collective-permute-start.28
  1857.4 5.8 collective-permute-start.29
  1896.8 4.4 collective-permute-start.4
  1917.4 34.6 %all-gather.1 = bf16[8,12,768]{2,1,0:T(8,128)(2,1)S(1)} all-gather(bf16[1,12,768]{2,1,0:T(8,128)(2,1)S(1)} %fusion.91), channel_id=1, replica_groups=mesh['section'=2,'shard'=8,'context'=4,'tensor'=2] {'context','tensor'}, dimensions={0}, use_global_device_ids=true | all-gather | bytes 165888 | tf_op jit(solution)/shard_map/all_gather | solution.py:294
  1955.8 35.5 %all-gather = bf16[8,12,2304]{2,1,0:T(8,128)(2,1)S(1)} all-gather(bf16[1,12,2304]{2,1,0:T(8,128)(2,1)S(1)} %fusion.90), channel_id=1, replica_groups=mesh['section'=2,'shard'=8,'context'=4,'tensor'=2] {'context','tensor'}, dimensions={0}, use_global_device_ids=true | all-gather | bytes 497664 | tf_op jit(solution)/shard_map/all_gather | solution.py:291
  1992.4 12.5 all_gather.78
  2005.8 12.5 all_gather.77
  (745 shorter events, 405.3 us)
Async XLA Ops:
  7.2 66.4 %all-gather.17.cloned.1.call-start = ((), (), s32[]{:S(2)}) async-start(), calls=%async_computation.8 | async-start | bytes 2654208 | tf_op jit(solution)/shard_map/all_gather | solution.py:74
  7.9 87.9 %all-gather.13.cloned.1.call-start = ((), (), s32[]{:S(2)}) async-start(), calls=%async_computation.6 | async-start | bytes 1327104 | tf_op jit(solution)/shard_map/all_gather | solution.py:72
  8.7 129.9 %all-gather.15.cloned.1.call-start = ((), (), s32[]{:S(2)}) async-start(), calls=%async_computation.7 | async-start | bytes 2654208 | tf_op jit(solution)/shard_map/all_gather | solution.py:73
  9.4 176.0 %all-gather.11.cloned.1.call-start = ((), (), s32[]{:S(2)}) async-start(), calls=%async_computation.5 | async-start | bytes 3981312 | tf_op jit(solution)/shard_map/all_gather | solution.py:71
  189.9 57.5 %all-gather.21.cloned.1.call-start = ((), (), s32[]{:S(2)}) async-start(), calls=%async_computation.12 | async-start | bytes 1769472 | tf_op jit(solution)/shard_map/while/body/eval_jaxpr/all_gather | solution.py:112
  198.1 100.4 %all-gather.19.cloned.1.call-start = ((), (), s32[]{:S(2)}) async-start(), calls=%async_computation.11 | async-start | bytes 1769472 | tf_op jit(solution)/shard_map/while/body/eval_jaxpr/all_gather | solution.py:115
  198.7 135.7 %reduce-scatter.20.cloned.1.call-start = ((), (), s32[]{:S(2)}) async-start(), calls=%async_computation.13 | async-start | bytes 589824 | tf_op jit(solution)/shard_map/while/body/eval_jaxpr/reduce_scatter | solution.py:131
  338.8 57.5 %all-gather.21.cloned.1.call-start = ((), (), s32[]{:S(2)}) async-start(), calls=%async_computation.12 | async-start | bytes 1769472 | tf_op jit(solution)/shard_map/while/body/eval_jaxpr/all_gather | solution.py:112
  347.0 100.5 %all-gather.19.cloned.1.call-start = ((), (), s32[]{:S(2)}) async-start(), calls=%async_computation.11 | async-start | bytes 1769472 | tf_op jit(solution)/shard_map/while/body/eval_jaxpr/all_gather | solution.py:115
  347.8 135.6 %reduce-scatter.20.cloned.1.call-start = ((), (), s32[]{:S(2)}) async-start(), calls=%async_computation.13 | async-start | bytes 589824 | tf_op jit(solution)/shard_map/while/body/eval_jaxpr/reduce_scatter | solution.py:131
  487.9 57.5 %all-gather.21.cloned.1.call-start = ((), (), s32[]{:S(2)}) async-start(), calls=%async_computation.12 | async-start | bytes 1769472 | tf_op jit(solution)/shard_map/while/body/eval_jaxpr/all_gather | solution.py:112
  496.1 100.4 %all-gather.19.cloned.1.call-start = ((), (), s32[]{:S(2)}) async-start(), calls=%async_computation.11 | async-start | bytes 1769472 | tf_op jit(solution)/shard_map/while/body/eval_jaxpr/all_gather | solution.py:115
  496.7 135.6 %reduce-scatter.20.cloned.1.call-start = ((), (), s32[]{:S(2)}) async-start(), calls=%async_computation.13 | async-start | bytes 589824 | tf_op jit(solution)/shard_map/while/body/eval_jaxpr/reduce_scatter | solution.py:131
  655.3 37.1 %reduce-scatter.22.cloned.1.call-start = ((), (), s32[]{:S(2)}) async-start(), calls=%async_computation.14 | async-start | bytes 589824 | tf_op jit(solution)/shard_map/while/body/eval_jaxpr/reduce_scatter | solution.py:192
  675.8 117.0 %reduce-scatter.24.cloned.1.call-start = ((), (), s32[]{:S(2)}) async-start(), calls=%async_computation.15 | async-start | bytes 3538944 | tf_op jit(solution)/shard_map/while
  802.4 36.7 %reduce-scatter.22.cloned.1.call-start = ((), (), s32[]{:S(2)}) async-start(), calls=%async_computation.14 | async-start | bytes 589824 | tf_op jit(solution)/shard_map/while/body/eval_jaxpr/reduce_scatter | solution.py:192
  823.1 116.3 %reduce-scatter.24.cloned.1.call-start = ((), (), s32[]{:S(2)}) async-start(), calls=%async_computation.15 | async-start | bytes 3538944 | tf_op jit(solution)/shard_map/while
  949.1 36.7 %reduce-scatter.22.cloned.1.call-start = ((), (), s32[]{:S(2)}) async-start(), calls=%async_computation.14 | async-start | bytes 589824 | tf_op jit(solution)/shard_map/while/body/eval_jaxpr/reduce_scatter | solution.py:192
  969.8 116.2 %reduce-scatter.24.cloned.1.call-start = ((), (), s32[]{:S(2)}) async-start(), calls=%async_computation.15 | async-start | bytes 3538944 | tf_op jit(solution)/shard_map/while
  1095.9 896.5 %reduce-scatter.18.cloned.1.call-start = ((), (), s32[]{:S(2)}) async-start(), calls=%async_computation.10 | async-start | bytes 2433024 | tf_op jit(solution)/shard_map/reduce_scatter | solution.py:308
  1100.6 905.2 %reduce-scatter.16.cloned.1.call-start = ((), (), s32[]{:S(2)}) async-start(), calls=%async_computation.9 | async-start | bytes 2433024 | tf_op jit(solution)/shard_map/reduce_scatter | solution.py:305
  1409.9 408.6 %collective-permute-start.18 = (bf16[16,768]{1,0:T(8,128)(2,1)S(1)}, bf16[16,768]{1,0:T(8,128)(2,1)S(1)}, u32[]{:S(2)}, u32[]{:S(2)}) collective-permute-start(bf16[16,768]{1,0:T(8,128)(2,1)S(1)} %convert.120), channel_id=1, source_target_pairs={{0,1},{1,2},{2,3},{3,4},{4,5},{5,6},{6,7},{7,8},{8,9},{9,10},{10,1... | collective-permute-start | bytes 73736
  1416.8 423.5 %collective-permute-start.19 = (bf16[16,768]{1,0:T(8,128)(2,1)S(1)}, bf16[16,768]{1,0:T(8,128)(2,1)S(1)}, u32[]{:S(2)}, u32[]{:S(2)}) collective-permute-start(bf16[16,768]{1,0:T(8,128)(2,1)S(1)} %convert.120), channel_id=1, source_target_pairs={{0,2},{1,3},{2,4},{3,5},{4,6},{5,7},{6,8},{7,9},{8,10},{9,11},{10,... | collective-permute-start | bytes 73736
  1429.1 414.2 %collective-permute-start.20 = (bf16[16,768]{1,0:T(8,128)(2,1)S(1)}, bf16[16,768]{1,0:T(8,128)(2,1)S(1)}, u32[]{:S(2)}, u32[]{:S(2)}) collective-permute-start(bf16[16,768]{1,0:T(8,128)(2,1)S(1)} %convert.120), channel_id=1, source_target_pairs={{0,3},{1,4},{2,5},{3,6},{4,7},{5,8},{6,9},{7,10},{8,11},{9,12},{10... | collective-permute-start | bytes 73736
  1444.3 400.3 %collective-permute-start.21 = (bf16[16,768]{1,0:T(8,128)(2,1)S(1)}, bf16[16,768]{1,0:T(8,128)(2,1)S(1)}, u32[]{:S(2)}, u32[]{:S(2)}) collective-permute-start(bf16[16,768]{1,0:T(8,128)(2,1)S(1)} %convert.120), channel_id=1, source_target_pairs={{0,4},{1,5},{2,6},{3,7},{4,8},{5,9},{6,10},{7,11},{8,12},{9,13},{1... | collective-permute-start | bytes 73736
  1447.3 366.9 %collective-permute-start.33 = (bf16[12,768]{1,0:T(8,128)(2,1)S(1)}, bf16[12,768]{1,0:T(8,128)(2,1)S(1)}, u32[]{:S(2)}, u32[]{:S(2)}) collective-permute-start(bf16[12,768]{1,0:T(8,128)(2,1)S(1)} %slice.90), channel_id=1, source_target_pairs={{0,16},{1,17},{2,18},{3,19},{4,20},{5,21},{6,22},{7,23},{8,24},{9,... | collective-permute-start | bytes 55304
  1814.3 31.7 %collective-permute-start.22 = (bf16[16,768]{1,0:T(8,128)(2,1)S(1)}, bf16[16,768]{1,0:T(8,128)(2,1)S(1)}, u32[]{:S(2)}, u32[]{:S(2)}) collective-permute-start(bf16[16,768]{1,0:T(8,128)(2,1)S(1)} %convert.120), channel_id=1, source_target_pairs={{0,5},{1,6},{2,7},{3,8},{4,9},{5,10},{6,11},{7,12},{8,13},{9,14},{... | collective-permute-start | bytes 73736
  1818.5 28.8 %collective-permute-start.23 = (bf16[16,768]{1,0:T(8,128)(2,1)S(1)}, bf16[16,768]{1,0:T(8,128)(2,1)S(1)}, u32[]{:S(2)}, u32[]{:S(2)}) collective-permute-start(bf16[16,768]{1,0:T(8,128)(2,1)S(1)} %convert.120), channel_id=1, source_target_pairs={{0,6},{1,7},{2,8},{3,9},{4,10},{5,11},{6,12},{7,13},{8,14},{9,15},... | collective-permute-start | bytes 73736
  1840.3 17.1 collective-permute-start.24
  1843.3 19.9 collective-permute-start.25
  1844.7 21.4 %collective-permute-start.26 = (bf16[16,768]{1,0:T(8,128)(2,1)S(1)}, bf16[16,768]{1,0:T(8,128)(2,1)S(1)}, u32[]{:S(2)}, u32[]{:S(2)}) collective-permute-start(bf16[16,768]{1,0:T(8,128)(2,1)S(1)} %convert.120), channel_id=1, source_target_pairs={{0,9},{1,10},{2,11},{3,12},{4,13},{5,14},{6,15},{7,16},{8,17},{9,1... | collective-permute-start | bytes 73736
  1846.0 23.3 %collective-permute-start.27 = (bf16[16,768]{1,0:T(8,128)(2,1)S(1)}, bf16[16,768]{1,0:T(8,128)(2,1)S(1)}, u32[]{:S(2)}, u32[]{:S(2)}) collective-permute-start(bf16[16,768]{1,0:T(8,128)(2,1)S(1)} %convert.120), channel_id=1, source_target_pairs={{0,10},{1,11},{2,12},{3,13},{4,14},{5,15},{6,16},{7,17},{8,18},{9,... | collective-permute-start | bytes 73736
  1847.3 23.6 %collective-permute-start.28 = (bf16[16,768]{1,0:T(8,128)(2,1)S(1)}, bf16[16,768]{1,0:T(8,128)(2,1)S(1)}, u32[]{:S(2)}, u32[]{:S(2)}) collective-permute-start(bf16[16,768]{1,0:T(8,128)(2,1)S(1)} %convert.120), channel_id=1, source_target_pairs={{0,11},{1,12},{2,13},{3,14},{4,15},{5,16},{6,17},{7,18},{8,19},{9,... | collective-permute-start | bytes 73736
  1857.4 15.9 collective-permute-start.29
  1873.3 13.9 collective-permute-start.10
  1874.7 14.6 collective-permute-start.11
  1876.4 14.7 collective-permute-start.12
  1880.4 14.5 collective-permute-start.13
  1887.3 16.9 collective-permute-start.15
  1889.3 18.2 collective-permute-start.16
  1891.1 20.6 %collective-permute-start.2 = (bf16[16,2304]{1,0:T(8,128)(2,1)S(1)}, bf16[16,2304]{1,0:T(8,128)(2,1)S(1)}, u32[]{:S(2)}, u32[]{:S(2)}) collective-permute-start(bf16[16,2304]{1,0:T(8,128)(2,1)S(1)} %convert.119), channel_id=1, source_target_pairs={{0,1},{1,2},{2,3},{3,4},{4,5},{5,6},{6,7},{7,8},{8,9},{9,10},{10,1... | collective-permute-start | bytes 221192
  1894.9 19.1 collective-permute-start.3
  1896.8 19.2 collective-permute-start.4
  1904.2 48.5 %collective-permute-start.5 = (bf16[16,2304]{1,0:T(8,128)(2,1)S(1)}, bf16[16,2304]{1,0:T(8,128)(2,1)S(1)}, u32[]{:S(2)}, u32[]{:S(2)}) collective-permute-start(bf16[16,2304]{1,0:T(8,128)(2,1)S(1)} %convert.119), channel_id=1, source_target_pairs={{0,4},{1,5},{2,6},{3,7},{4,8},{5,9},{6,10},{7,11},{8,12},{9,13},{1... | collective-permute-start | bytes 221192
  1907.5 45.2 %collective-permute-start.6 = (bf16[16,2304]{1,0:T(8,128)(2,1)S(1)}, bf16[16,2304]{1,0:T(8,128)(2,1)S(1)}, u32[]{:S(2)}, u32[]{:S(2)}) collective-permute-start(bf16[16,2304]{1,0:T(8,128)(2,1)S(1)} %convert.119), channel_id=1, source_target_pairs={{0,5},{1,6},{2,7},{3,8},{4,9},{5,10},{6,11},{7,12},{8,13},{9,14},{... | collective-permute-start | bytes 221192
  1911.7 41.0 %collective-permute-start.7 = (bf16[16,2304]{1,0:T(8,128)(2,1)S(1)}, bf16[16,2304]{1,0:T(8,128)(2,1)S(1)}, u32[]{:S(2)}, u32[]{:S(2)}) collective-permute-start(bf16[16,2304]{1,0:T(8,128)(2,1)S(1)} %convert.119), channel_id=1, source_target_pairs={{0,6},{1,7},{2,8},{3,9},{4,10},{5,11},{6,12},{7,13},{8,14},{9,15},... | collective-permute-start | bytes 221192
  1914.0 38.7 %collective-permute-start.8 = (bf16[16,2304]{1,0:T(8,128)(2,1)S(1)}, bf16[16,2304]{1,0:T(8,128)(2,1)S(1)}, u32[]{:S(2)}, u32[]{:S(2)}) collective-permute-start(bf16[16,2304]{1,0:T(8,128)(2,1)S(1)} %convert.119), channel_id=1, source_target_pairs={{0,7},{1,8},{2,9},{3,10},{4,11},{5,12},{6,13},{7,14},{8,15},{9,16}... | collective-permute-start | bytes 221192
  1915.9 36.8 %collective-permute-start.9 = (bf16[16,2304]{1,0:T(8,128)(2,1)S(1)}, bf16[16,2304]{1,0:T(8,128)(2,1)S(1)}, u32[]{:S(2)}, u32[]{:S(2)}) collective-permute-start(bf16[16,2304]{1,0:T(8,128)(2,1)S(1)} %convert.119), channel_id=1, source_target_pairs={{0,8},{1,9},{2,10},{3,11},{4,12},{5,13},{6,14},{7,15},{8,16},{9,17... | collective-permute-start | bytes 221192
  (152 other events, 2965.5 us)
Sparse Core Ops, SparseCore 0:
  9.7 45.4 all-gather.16
  56.8 38.9 all-gather.12
  97.5 41.0 all-gather.14
  140.1 45.2 all-gather.10
  198.2 49.1 all-gather.20
  250.1 48.3 all-gather.18
  319.1 15.2 reduce-scatter.19
  347.2 49.1 all-gather.20
  399.2 48.3 all-gather.18
  468.1 15.2 reduce-scatter.19
  496.2 49.1 all-gather.20
  548.1 48.3 all-gather.18
  617.0 15.2 reduce-scatter.19
  675.9 16.5 reduce-scatter.21
  713.8 78.8 reduce-scatter.23
  823.3 15.8 reduce-scatter.21
  860.5 78.8 reduce-scatter.23
  969.9 15.8 reduce-scatter.21
  1007.2 78.7 reduce-scatter.23
  1100.7 167.9 reduce-scatter.17
  1271.1 163.2 reduce-scatter.15
where the time goes:
time: 2040 us; the launch traced here: 2030 us
  blocking collectives  886 us (43%)
  waiting for transfers between devices  613 us (30%)
  local copies, waits for them, and re-layouts  171 us (8%)
  starting transfers between devices  131 us (6%)
  matrix products  126 us (6%)
  other arithmetic  65.3 us (3%)
    unnamed x2, blocking collectives  639 us
    while x18, waiting for transfers between devices  213 us
    all_gather x3, waiting for transfers between devices, forward_step(): lax.all_gather(projected[:, 2 * feat_width:], ('context', 'tensor'), axis...  136 us
    all_gather x3, waiting for transfers between devices, forward_step(): lax.all_gather(projected[:, feat_width:2 * feat_width], ('context', 'tens...  133 us
    unnamed x32, starting transfers between devices  121 us
    dynamic_update_slice x39, local copies, waits for them, and re-layouts, per_device(): _, fwd_kept = lax.scan(forward_step, empty_rows, step_ids)  52.2 us
    all_gather x1, waiting for transfers between devices, per_device(): lax.all_gather(w_qkv, 'shard', axis=1, tiled=True)  46.8 us
    all_gather x1, waiting for transfers between devices, per_device(): lax.all_gather(w_fc, 'shard', axis=1, tiled=True)  42.8 us
  transfers between devices with their start and end apart: 59, of which 24 were waited for; matrix products, arithmetic and copies ran while one was open for 23% of the time, Pallas kernels for 0%

commit v1 on v0

v1 whole, which is shorter than its diff:
```python
import functools
import math

import jax
import jax.numpy as jnp
from jax import lax
from jax.experimental import pallas as pl
from jax.experimental.pallas import tpu as pltpu
from jax.sharding import PartitionSpec as P

HEAD_DIM = 64
EPSILON = 1e-05
MASKED = -1000000000.0
MESH = pl.DeviceIdType.MESH
BF16 = jnp.bfloat16
F32 = jnp.float32
ANY = pl.BlockSpec(memory_space=pl.ANY)
VMEM = pl.BlockSpec(memory_space=pltpu.VMEM)


class Copies:
    def __init__(self, send_sems, recv_sems):
        self.send_sems, self.recv_sems, self.made = send_sems, recv_sems, []

    def push(self, src, dst, device_id):
        index = len(self.made)
        copy = pltpu.make_async_remote_copy(
            src_ref=src,
            dst_ref=dst,
            send_sem=self.send_sems.at[index],
            recv_sem=self.recv_sems.at[index],
            device_id=device_id,
            device_id_type=MESH,
        )
        copy.start()
        self.made.append(copy)
        return copy

    def finish(self):
        for copy in self.made:
            copy.wait_send()


def greet(peers):
    barrier = pltpu.get_barrier_semaphore()
    for peer in peers:
        pl.semaphore_signal(barrier, inc=1, device_id=peer, device_id_type=MESH)
    pl.semaphore_wait(barrier, len(peers))


def call_remote(body, out_shape, copies, collective_id, args, scratch=(), locals_=1, specs=None, vmem=None):
    in_specs, out_specs = specs if specs else ([ANY] * len(args), jax.tree.map(lambda _: ANY, out_shape))
    return pl.pallas_call(
        body,
        out_shape=out_shape,
        in_specs=in_specs,
        out_specs=out_specs,
        scratch_shapes=[
            *scratch,
            pltpu.SemaphoreType.DMA((copies,)),
            pltpu.SemaphoreType.DMA((copies,)),
            pltpu.SemaphoreType.DMA((locals_,)),
        ],
        compiler_params=pltpu.CompilerParams(
            collective_id=collective_id, has_side_effects=True, vmem_limit_bytes=vmem
        ),
    )(*args)


def place():
    shard = lax.axis_index("shard")
    return lax.axis_index("section"), shard // 4, lax.rem(shard, 4)


AG_COPIES = 64


def weights_body(split, own_ref, all_ref, send_sems, recv_sems, local_sems):
    section, row, col = place()
    columns = own_ref.shape[1]
    right, left, far = lax.rem(col + 1, 4), lax.rem(col + 3, 4), lax.rem(col + 2, 4)
    to_right = {"shard": row * 4 + right}
    to_left = {"shard": row * 4 + left}
    other = 1 - row
    to_row = {"shard": other * 4 + col}
    to_core = {"section": 1 - section}
    greet([to_right, to_left, to_row, to_core])
    copies = Copies(send_sems, recv_sems)
    parts = (pl.ds(0, split), pl.ds(split, columns - split))
    half = own_ref.shape[0] // 2
    rows = (pl.ds(0, half), pl.ds(half, half))

    def slot(a_row, a_col, part, which=None):
        shard = a_row * 4 + a_col
        if which is None:
            return all_ref.at[section, shard, :, parts[part]]
        return all_ref.at[section, shard, rows[which], parts[part]]

    own_a, own_b = own_ref.at[:, parts[0]], own_ref.at[:, parts[1]]
    b_row = copies.push(own_b, slot(row, col, 1), to_row)
    a_right = copies.push(own_a, slot(row, col, 0), to_right)
    a_left = copies.push(own_a, slot(row, col, 0), to_left)
    a_row = copies.push(own_a, slot(row, col, 0), to_row)
    b_right = copies.push(own_b, slot(row, col, 1), to_right)
    b_left = copies.push(own_b, slot(row, col, 1), to_left)
    c_own = copies.push(own_ref, all_ref.at[section, row * 4 + col], to_core)
    mine = pltpu.make_async_copy(own_ref, all_ref.at[section, row * 4 + col], local_sems.at[0])
    mine.start()
    cores = [c_own]

    def share(ref):
        cores.append(copies.push(ref, ref, to_core))

    a_right.wait_recv()
    ref = slot(row, left, 0)
    a_far_right = copies.push(slot(row, left, 0, 0), slot(row, left, 0, 0), to_right)
    a_row_left = copies.push(ref, ref, to_row)
    a_left.wait_recv()
    ref2 = slot(row, right, 0)
    a_far_left = copies.push(slot(row, right, 0, 1), slot(row, right, 0, 1), to_left)
    a_row_right = copies.push(ref2, ref2, to_row)
    b_row.wait_recv()
    ref3 = slot(other, col, 1)
    b_or = copies.push(ref3, ref3, to_right)
    b_ol = copies.push(ref3, ref3, to_left)
    share(ref)
    share(ref2)
    share(ref3)
    a_far_right.wait_recv()
    a_far_left.wait_recv()
    ref = slot(row, far, 0)
    a_row_far = copies.push(ref, ref, to_row)
    share(ref)
    b_right.wait_recv()
    b_far_right = copies.push(slot(row, left, 1, 0), slot(row, left, 1, 0), to_right)
    share(slot(row, left, 1))
    b_left.wait_recv()
    b_far_left = copies.push(slot(row, right, 1, 1), slot(row, right, 1, 1), to_left)
    share(slot(row, right, 1))
    a_row.wait_recv()
    share(slot(other, col, 0))
    b_or.wait_recv()
    bo_far_right = copies.push(slot(other, left, 1, 0), slot(other, left, 1, 0), to_right)
    share(slot(other, left, 1))
    b_ol.wait_recv()
    bo_far_left = copies.push(slot(other, right, 1, 1), slot(other, right, 1, 1), to_left)
    share(slot(other, right, 1))
    a_row_left.wait_recv()
    share(slot(other, left, 0))
    a_row_right.wait_recv()
    share(slot(other, right, 0))
    b_far_right.wait_recv()
    b_far_left.wait_recv()
    share(slot(row, far, 1))
    a_row_far.wait_recv()
    share(slot(other, far, 0))
    bo_far_right.wait_recv()
    bo_far_left.wait_recv()
    share(slot(other, far, 1))
    for copy in cores:
        copy.wait_recv()
    copies.finish()
    mine.wait()


def gather_weights(own):
    depth, columns = own.shape
    return call_remote(
        functools.partial(weights_body, 2688),
        jax.ShapeDtypeStruct((2, 8, depth, columns), own.dtype),
        AG_COPIES,
        0,
        (own,),
    )


def span_peers():
    context, tensor = lax.axis_index("context"), lax.axis_index("tensor")
    span = context * 2 + tensor
    peers = []
    for step in range(1, 8):
        peer = lax.rem(span + step, 8)
        peers.append((peer, peer // 2, lax.rem(peer, 2)))
    return context, tensor, span, peers


def heads_body(by_span, q_ref, kv_ref, q_out, kv_out, send_sems, recv_sems, local_sems):
    context, tensor, span, peers = span_peers()
    greet([{"context": c, "tensor": t} for _, c, t in peers])
    copies = Copies(send_sems, recv_sems)
    for peer, c, t in peers:
        copies.push(
            kv_ref.at[peer if by_span else c], kv_out.at[span], {"context": c, "tensor": t}
        )
    for step in range(1, 4):
        c = lax.rem(context + step, 4)
        copies.push(q_ref.at[c], q_out.at[context], {"context": c})
    own = [
        pltpu.make_async_copy(q_ref.at[context], q_out.at[context], local_sems.at[0]),
        pltpu.make_async_copy(
            kv_ref.at[span if by_span else context], kv_out.at[span], local_sems.at[1]
        ),
    ]
    for copy in own:
        copy.start()
    for copy in copies.made:
        copy.wait_recv()
    copies.finish()
    for copy in own:
        copy.wait()


def exchange_heads(q_parts, kv_parts, by_span):
    return call_remote(
        functools.partial(heads_body, by_span),
        (
            jax.ShapeDtypeStruct(q_parts.shape, q_parts.dtype),
            jax.ShapeDtypeStruct((8, *kv_parts.shape[1:]), kv_parts.dtype),
        ),
        10,
        1 if by_span else 2,
        (q_parts, kv_parts),
        locals_=2,
    )


def context_body(in_ref, out_ref, send_sems, recv_sems, local_sems):
    context = lax.axis_index("context")
    peers = [lax.rem(context + step, 4) for step in range(1, 4)]
    greet([{"context": c} for c in peers])
    copies = Copies(send_sems, recv_sems)
    for c in peers:
        copies.push(in_ref.at[c], out_ref.at[context], {"context": c})
    own = pltpu.make_async_copy(in_ref.at[context], out_ref.at[context], local_sems.at[0])
    own.start()
    for copy in copies.made:
        copy.wait_recv()
    copies.finish()
    own.wait()


def exchange_context(parts):
    return call_remote(
        context_body, jax.ShapeDtypeStruct(parts.shape, parts.dtype), 3, 3, (parts,)
    )


def pair_body(in_ref, out_ref, send_sems, recv_sems, local_sems):
    peer = {"tensor": 1 - lax.axis_index("tensor")}
    greet([peer])
    copies = Copies(send_sems, recv_sems)
    copies.push(in_ref, out_ref, peer)
    copies.made[0].wait_recv()
    copies.finish()


def exchange_pair(rows):
    return call_remote(pair_body, jax.ShapeDtypeStruct(rows.shape, rows.dtype), 1, 4, (rows,))


BLOCK = 16


def add_rows(dst, terms, rows, cast=BF16):
    def step(index, _):
        at = pl.ds(pl.multiple_of(index * BLOCK, BLOCK), BLOCK)
        total = terms[0][at, :].astype(F32)
        for term in terms[1:]:
            total = total + term[at, :].astype(F32)
        dst[at, :] = total.astype(cast)
        return 0

    lax.fori_loop(0, rows // BLOCK, step, 0)


def grads_body(
    ga, gb, gn, out_a, out_b, out_n, a1, a2, a3, b1, b2, b3, n1, n2, za, zb, fa, fb,
    send_sems, recv_sems, local_sems,
):
    _, row, col = place()
    other = 1 - row
    right, left, far = lax.rem(col + 1, 4), lax.rem(col + 3, 4), lax.rem(col + 2, 4)
    to_right = {"shard": row * 4 + right}
    to_left = {"shard": row * 4 + left}
    to_row = {"shard": other * 4 + col}
    shard = row * 4 + col
    context, tensor, span, spans = span_peers()
    shard_peers = [lax.rem(shard + step, 8) for step in range(1, 8)]
    greet(
        [{"shard": peer} for peer in shard_peers]
        + [{"context": c, "tensor": t} for _, c, t in spans]
    )
    copies = Copies(send_sems, recv_sems)
    depth, width = ga.shape[1], ga.shape[2]
    half = depth // 2
    lower, upper = pl.ds(0, half), pl.ds(half, half)

    a_far_r = copies.push(ga.at[far], a1.at[0], to_right)
    a_far_l = copies.push(ga.at[4 + far], a1.at[1], to_left)
    b_far = copies.push(gb.at[other * 4 + far], b1.at[0], to_row)
    b_right = copies.push(gb.at[other * 4 + right], b1.at[1], to_row)
    b_left = copies.push(gb.at[other * 4 + left], b1.at[2], to_row)
    b_own = copies.push(gb.at[other * 4 + col], b1.at[3], to_row)
    a_plain_r = copies.push(ga.at[4 + right], a2.at[1], to_right)
    a_plain_l = copies.push(ga.at[left], a3.at[0], to_left)
    norms = [copies.push(gn.at[peer], n1.at[shard], {"shard": peer}) for peer in shard_peers]

    a_far_r.wait_recv()
    add_rows(a1.at[0], [a1.at[0], ga.at[right]], depth)
    a_sum_r = copies.push(a1.at[0], a2.at[0], to_right)
    a_far_l.wait_recv()
    add_rows(a1.at[1], [a1.at[1], ga.at[4 + left]], depth)
    a_sum_l = copies.push(a1.at[1], a3.at[1], to_left)

    b_far.wait_recv()
    add_rows(b1.at[0], [b1.at[0], gb.at[row * 4 + far]], depth)
    b_far_r = copies.push(b1.at[0, lower], b2.at[0], to_right)
    b_far_l = copies.push(b1.at[0, upper], b2.at[1], to_left)
    b_right.wait_recv()
    add_rows(b1.at[1], [b1.at[1], gb.at[row * 4 + right]], depth)
    b_left.wait_recv()
    add_rows(b1.at[2], [b1.at[2], gb.at[row * 4 + left]], depth)

    a_plain_r.wait_recv()
    a_plain_l.wait_recv()
    a_sum_r.wait_recv()
    a_sum_l.wait_recv()
    add_rows(a2.at[other], [a2.at[other], a3.at[other], ga.at[other * 4 + col]], depth)
    a_row = copies.push(a2.at[other], a2.at[2], to_row)
    add_rows(a2.at[row], [a2.at[row], a3.at[row], ga.at[row * 4 + col]], depth)

    b_far_r.wait_recv()
    add_rows(b1.at[1, lower], [b1.at[1, lower], b2.at[0]], half)
    b_sum_r = copies.push(b1.at[1], b3.at[0], to_right)
    b_far_l.wait_recv()
    add_rows(b1.at[2, upper], [b1.at[2, upper], b2.at[1]], half)
    b_sum_l = copies.push(b1.at[2], b3.at[1], to_left)

    n1[shard] = gn[shard]
    for copy in norms:
        copy.wait_recv()
    n2[span] = jnp.sum(n1[...], axis=0)
    norms2 = [
        copies.push(n2.at[span], n2.at[span], {"context": c, "tensor": t}) for _, c, t in spans
    ]

    a_row.wait_recv()
    wide = width // 8
    a_own = a2.at[row]
    add_rows(a_own, [a_own, a2.at[2]], depth)
    a_piece = [
        copies.push(
            a_own.at[:, pl.ds(pl.multiple_of(peer * wide, 128), wide)],
            za.at[span],
            {"context": c, "tensor": t},
        )
        for peer, c, t in spans
    ]
    b_own.wait_recv()
    b_sum_r.wait_recv()
    b_sum_l.wait_recv()
    add_rows(
        b1.at[3], [b1.at[3], gb.at[row * 4 + col], b3.at[0], b3.at[1]], depth
    )
    wide_b = width // 4
    contexts = [lax.rem(context + step, 4) for step in range(1, 4)]
    b_piece = [
        copies.push(
            b1.at[3, :, pl.ds(pl.multiple_of(c * wide_b, 128), wide_b)],
            zb.at[context],
            {"context": c},
        )
        for c in contexts
    ]
    za[span] = a_own[:, pl.ds(pl.multiple_of(span * wide, 128), wide)]
    zb[context] = b1[3, :, pl.ds(pl.multiple_of(context * wide_b, 128), wide_b)]
    for copy in a_piece:
        copy.wait_recv()
    add_rows(fa.at[span], [za.at[index] for index in range(8)], depth)
    a_back = [
        copies.push(fa.at[span], fa.at[span], {"context": c, "tensor": t}) for _, c, t in spans
    ]
    for copy in b_piece:
        copy.wait_recv()
    add_rows(fb.at[context], [zb.at[index] for index in range(4)], depth)
    b_back = [copies.push(fb.at[context], fb.at[context], {"context": c}) for c in contexts]
    for copy in norms2:
        copy.wait_recv()
    out_n[...] = jnp.sum(n2[...], axis=0)
    for copy in a_back:
        copy.wait_recv()
    for index in range(8):
        out_a[:, index * wide : (index + 1) * wide] = fa[index].astype(F32)
    for copy in b_back:
        copy.wait_recv()
    for index in range(4):
        out_b[:, index * wide_b : (index + 1) * wide_b] = fb[index].astype(F32)
    copies.finish()


def reduce_grads(ga, gb, gn):
    _, depth, width = ga.shape
    half = depth // 2
    return call_remote(
        grads_body,
        (
            jax.ShapeDtypeStruct((depth, width), F32),
            jax.ShapeDtypeStruct((depth, width), F32),
            jax.ShapeDtypeStruct(gn.shape[1:], F32),
        ),
        64,
        5,
        (ga, gb, gn),
        scratch=[
            pltpu.VMEM((2, depth, width), BF16),
            pltpu.VMEM((3, depth, width), BF16),
            pltpu.VMEM((2, depth, width), BF16),
            pltpu.VMEM((4, depth, width), BF16),
            pltpu.VMEM((2, half, width), BF16),
            pltpu.VMEM((2, depth, width), BF16),
            pltpu.VMEM(gn.shape, F32),
            pltpu.VMEM(gn.shape, F32),
            pltpu.VMEM((8, depth, width // 8), BF16),
            pltpu.VMEM((4, depth, width // 4), BF16),
            pltpu.VMEM((8, depth, width // 8), BF16),
            pltpu.VMEM((4, depth, width // 4), BF16),
        ],
        specs=([VMEM] * 3, (VMEM, VMEM, VMEM)),
        vmem=48 * 1024 * 1024,
    )


def layer_norm(values, gain_vec, bias_vec):
    row_mean = jnp.mean(values, -1, keepdims=True)
    centred = values - row_mean
    variance = jnp.mean(centred * centred, -1, keepdims=True)
    return centred * lax.rsqrt(variance + EPSILON) * gain_vec + bias_vec


def smooth_unit(values):
    return jax.nn.gelu(values, approximate=True)


def dot(first, second):
    return jnp.dot(first, second, preferred_element_type=F32)


def dot_tn(first, second):
    return lax.dot_general(first, second, (((0,), (0,)), ((), ())), preferred_element_type=F32)


def dot_nt(first, second):
    return lax.dot_general(first, second, (((1,), (1,)), ((), ())), preferred_element_type=F32)


def to_groups(rows):
    return rows.reshape(rows.shape[0], 4, -1).transpose(1, 0, 2)


def from_groups(groups):
    return groups.transpose(1, 0, 2).reshape(groups.shape[1], -1)


def heads_of(rows):
    return rows.reshape(rows.shape[0], -1, HEAD_DIM)


def per_device(
    block_input, cotangent, segment_ids, w_qkv, w_out, w_fc, w_proj, norm_gains, norm_biases
):
    section = lax.axis_index("section")
    tensor = lax.axis_index("tensor")
    tokens, width = block_input.shape[2:]
    units = w_fc.shape[2]
    depth = w_qkv.shape[1]
    group = width // 4
    scale = 1.0 / math.sqrt(HEAD_DIM)

    vectors = jnp.concatenate([norm_gains[0], norm_biases[0]], 0)
    vectors = jnp.pad(vectors.T, ((0, 0), (0, 124)))
    own = jnp.concatenate([w_qkv[0], w_out[0], w_fc[0], w_proj[0].T, vectors], 1)
    full = gather_weights(own).reshape(2, width, -1)

    def weights(block):
        edges = [0, 3 * width, 4 * width, 4 * width + units, 4 * width + 2 * units]
        pieces = [full[block, :, edges[k] : edges[k + 1]] for k in range(4)]
        norms = full[block, :, edges[4] : edges[4] + 4].T.astype(F32)
        return (*pieces, norms)

    def mine(stacked):
        return lax.dynamic_index_in_dim(stacked, section, 0, keepdims=False)

    seg_keys = mine(segment_ids)[0]
    seg_queries = lax.dynamic_index_in_dim(
        seg_keys.reshape(4, 2, tokens), tensor, 1, keepdims=False
    ).reshape(-1)
    key_pos = jnp.arange(8 * tokens)
    query_pos = lax.dynamic_index_in_dim(
        key_pos.reshape(4, 2, tokens), tensor, 1, keepdims=False
    ).reshape(-1)
    allowed = (key_pos[None, :] <= query_pos[:, None]) & (
        seg_keys[None, :] == seg_queries[:, None]
    )

    def masked_scores(query, keys):
        raw = jnp.einsum("qhd,khd->hqk", query, keys, preferred_element_type=F32)
        return jnp.where(allowed[None], raw * scale, MASKED)

    def forward(block, entry):
        qkv, out, fc, proj, norms = weights(block)
        inputs = entry.astype(F32)
        normed = layer_norm(inputs, norms[0], norms[2]).astype(BF16)
        projected = dot(normed, qkv).astype(BF16)
        q_parts = to_groups(projected[:, :width])
        kv_parts = jnp.concatenate(
            [to_groups(projected[:, width : 2 * width]), to_groups(projected[:, 2 * width :])], 2
        )
        q_all, kv_all = exchange_heads(q_parts, kv_parts, False)
        query = heads_of(q_all.reshape(-1, group))
        kv_all = kv_all.reshape(-1, 2 * group)
        keys, values = heads_of(kv_all[:, :group]), heads_of(kv_all[:, group:])
        masked = masked_scores(query, keys)
        totals = jax.nn.logsumexp(masked, axis=-1)
        probs_low = jnp.exp(masked - totals[..., None]).astype(BF16)
        mixed = jnp.einsum("hqk,khd->qhd", probs_low, values, preferred_element_type=F32)
        mixed = mixed.reshape(4, tokens, group).astype(BF16)
        mixed = from_groups(exchange_context(mixed))
        resid = inputs + dot(mixed, out)
        inner = layer_norm(resid, norms[1], norms[3]).astype(BF16)
        inner_all = jnp.concatenate([inner, exchange_pair(inner)], 0)
        upward = dot(inner_all, fc)
        active = smooth_unit(upward).astype(BF16)
        down = dot_nt(active, proj)
        down = down[:tokens] + exchange_pair(down[tokens:].astype(BF16)).astype(F32)
        sent = (resid + down).astype(BF16)
        return sent, (entry, normed, query, keys, values, totals, mixed, resid, inner_all, upward, active)

    def backward(block, incoming, kept):
        qkv, out, fc, proj, norms = weights(block)
        entry, normed, query, keys, values, totals, mixed, resid, inner_all, upward, active = kept
        incoming_all = jnp.concatenate([incoming, exchange_pair(incoming)], 0)
        active_grad = dot(incoming_all, proj)
        _, unit_pull = jax.vjp(smooth_unit, upward)
        upward_grad = unit_pull(active_grad)[0].astype(BF16)
        inner_grad = dot_nt(upward_grad, fc)
        inner_grad = inner_grad[:tokens] + exchange_pair(inner_grad[tokens:].astype(BF16)).astype(F32)
        _, late_pull = jax.vjp(layer_norm, resid, norms[1], norms[3])
        resid_part, gain_late, bias_late = late_pull(inner_grad)
        resid_grad = incoming.astype(F32) + resid_part
        resid_low = resid_grad.astype(BF16)
        mixed_grad = dot_nt(resid_low, out).astype(BF16)
        mixed_heads = heads_of(exchange_context(to_groups(mixed_grad)).reshape(-1, group))
        probs = jnp.exp(masked_scores(query, keys) - totals[..., None])
        probs_low = probs.astype(BF16)
        prob_grad = jnp.einsum("qhd,khd->hqk", mixed_heads, values, preferred_element_type=F32)
        centre = jnp.sum(probs * prob_grad, -1, keepdims=True)
        score_grad = (probs * (prob_grad - centre)).astype(BF16)
        q_grad = jnp.einsum("hqk,khd->qhd", score_grad, keys, preferred_element_type=F32) * scale
        k_grad = jnp.einsum("hqk,qhd->khd", score_grad, query, preferred_element_type=F32) * scale
        v_grad = jnp.einsum("hqk,qhd->khd", probs_low, mixed_heads, preferred_element_type=F32)
        kv_grad = jnp.concatenate(
            [k_grad.reshape(8, tokens, group), v_grad.reshape(8, tokens, group)], 2
        )
        q_back, kv_back = exchange_heads(
            q_grad.reshape(4, tokens, group).astype(BF16), kv_grad.astype(BF16), True
        )
        kv_back = jnp.sum(kv_back.reshape(4, 2, tokens, 2 * group).astype(F32), 1).astype(BF16)
        projected_grad = jnp.concatenate(
            [
                from_groups(q_back),
                from_groups(kv_back[:, :, :group]),
                from_groups(kv_back[:, :, group:]),
            ],
            1,
        )
        normed_grad = dot_nt(projected_grad, qkv)
        _, early_pull = jax.vjp(layer_norm, entry.astype(F32), norms[0], norms[2])
        input_part, gain_early, bias_early = early_pull(normed_grad)
        sent_grad = (resid_grad + input_part).astype(BF16)
        vector_grads = jnp.stack([gain_early, gain_late, bias_early, bias_late])
        operands = (
            normed, projected_grad, mixed, resid_low, inner_all, upward_grad, incoming_all, active,
            vector_grads,
        )
        return sent_grad, operands

    first, kept_first = forward(0, mine(block_input)[0])
    second, kept_second = forward(1, first)
    grad_second, operands_second = backward(1, mine(cotangent)[0], kept_second)
    grad_first, operands_first = backward(0, grad_second, kept_first)

    def swap(of_first, of_second):
        keep = jnp.where(section == 0, of_first, of_second)
        send = jnp.where(section == 0, of_second, of_first)
        return keep, lax.ppermute(send, "section", [(0, 1), (1, 0)])

    def both(of_first, of_second):
        keep, got = swap(of_first, of_second)
        return jnp.concatenate([keep, got], 0)

    def in_order(of_first, of_second):
        keep, got = swap(of_first, of_second)
        return jnp.where(section == 0, jnp.stack([keep, got]), jnp.stack([got, keep]))

    normed, projected_grad, mixed, resid_low, inner_all, upward_grad, incoming_all, active = (
        both(one, two) for one, two in zip(operands_first[:-1], operands_second[:-1])
    )
    keep, got = swap(operands_first[-1], operands_second[-1])
    vector_grads = keep + got
    block_outputs = in_order(first, second)
    input_grads = in_order(grad_first, grad_second)

    ga = jnp.concatenate([dot_tn(normed, projected_grad), dot_tn(mixed, resid_low)], 1)
    gb = jnp.concatenate([dot_tn(inner_all, upward_grad), dot_tn(incoming_all, active)], 1)
    gn = vector_grads.reshape(4, 8, depth).transpose(1, 0, 2)
    gn = jnp.pad(gn, ((0, 0), (0, 4), (0, 128 - depth)))
    out_a, out_b, out_n = reduce_grads(
        ga.astype(BF16).reshape(8, depth, -1), gb.astype(BF16).reshape(8, depth, -1), gn
    )
    out_n = out_n[:4, :depth]
    return (
        block_outputs[None, :, None],
        input_grads[None, :, None],
        out_a[None, :, : 3 * width],
        out_a[None, :, 3 * width :],
        out_b[None, :, :units],
        out_b[:, units:].T[None],
        out_n[None, :2],
        out_n[None, 2],
        out_n[None, 3],
    )


def solution(mesh):
    in_specs = (
        P(None, "shard", ("context", "tensor"), None),
        P(None, "shard", ("context", "tensor"), None),
        P(None, "shard", None),
        P("section", "shard", None),
        P("section", "shard", None),
        P("section", "shard", "tensor"),
        P("section", "tensor", "shard"),
        P("section", None, "shard"),
        P("section", None, "shard"),
    )
    out_specs = (
        P("section", None, "shard", ("context", "tensor"), None),
        P("section", None, "shard", ("context", "tensor"), None),
        P("section", "shard", None),
        P("section", "shard", None),
        P("section", "shard", "tensor"),
        P("section", "tensor", "shard"),
        P("section", None, "shard"),
        P("section", "shard"),
        P("section", "shard"),
    )
    return jax.shard_map(
        per_device, mesh=mesh, in_specs=in_specs, out_specs=out_specs, check_vma=False
    )
```

time: 2040 us -> 518 us (0.25)
  blocking collectives: 886 us -> 0 us
  waiting for transfers between devices: 613 us -> 0.03 us
  Pallas kernels: 0 us -> 332 us
  starting transfers between devices: 131 us -> 2.41 us
  local copies, waits for them, and re-layouts: 171 us -> 45.9 us
  matrix products: 126 us -> 80.3 us
    unnamed x2 -> x0, blocking collectives: 639 us -> none
    all_gather x10 -> x0, waiting for transfers between devices: 377 us -> none  [the longest x3 136 us: forward_step(): lax.all_gather(projected[:, 2 * feat_width:], ('context', 'tensor'), axis...]
    pallas_call x0 -> x18, Pallas kernels: none -> 332 us  [call_remote(): pl.pallas_call(body, out_shape=out_shape, in_specs=in_specs, out_specs=ou...]
    all_gather x14 -> x0, blocking collectives: 246 us -> none  [the longest x1 35.5 us: per_device(): lax.all_gather(qkv_part.astype(jnp.bfloat16), ('context', 'tensor'), axis...]
    while x18 -> x0, waiting for transfers between devices: 213 us -> none
    unnamed x32 -> x0, starting transfers between devices: 121 us -> none
    dynamic_update_slice x45 -> x0, local copies, waits for them, and re-layouts: 55.6 us -> none  [the longest x39 52.2 us: per_device(): _, fwd_kept = lax.scan(forward_step, empty_rows, step_ids)]
    dot_general x49 -> x32, matrix products: 126 us -> 80.3 us  [the longest x8 25.9 us: dot(): return jnp.dot(first, second, preferred_element_type=F32)]
  transfers between devices with their start and end apart: 59 -> 11, of which waited for: 24 -> 0; matrix products, arithmetic and copies ran while one was open for 23% -> 21% of each run, Pallas kernels for 0% -> 19%
where the time goes in v1:
time: 518 us; the launch traced here: 511 us
  Pallas kernels  332 us (64%)
  matrix products  80.3 us (16%)
  other arithmetic  48 us (9%)
  local copies, waits for them, and re-layouts  45.9 us (9%)
    pallas_call x18, Pallas kernels, call_remote(): pl.pallas_call(body, out_shape=out_shape, in_specs=in_specs, out_specs=ou...  332 us
    dot_general x8, matrix products, dot(): return jnp.dot(first, second, preferred_element_type=F32)  25.9 us
    dot_general x8, matrix products, dot_nt(): lax.dot_general(first, second, (((1,), (1,)), ((), ())), preferred_elemen...  22.7 us
  transfers between devices with their start and end apart: 11, of which 0 were waited for; matrix products, arithmetic and copies ran while one was open for 21% of the time, Pallas kernels for 19%

profile of v1, /device:TPU:0, one launch (start us, length us, event | category | flops | bytes accessed | tf_op | source)
XLA Modules:
  0.0 511.2 jit_solution(14230193470158139389)
XLA Ops:
  7.8 69.2 %shard_map.160 = bf16[2,8,96,6272]{3,2,1,0:T(8,128)(2,1)} custom-call(bf16[96,6272]{1,0:T(8,128)(2,1)} %copy-done.19), custom_call_target="tpu_custom_call" | custom-call | tf_op jit(solution)/shard_map/pallas_call | solution.py:53
  78.6 2.7 convolution_convert_fusion.2
  83.9 20.7 %shard_map.161 = (bf16[4,128,192]{2,1,0:T(8,128)(2,1)}, bf16[8,128,384]{2,1,0:T(8,128)(2,1)}) custom-call(bf16[4,128,192]{2,1,0:T(8,128)(2,1)} %bitcast.320, bf16[4,128,384]{2,1,0:T(8,128)(2,1)} %pad_maximum_fusion.6.kv_ref), custom_call_target="tpu_custom_call" | custom-call | tf_op jit(solution)/shard_map/pallas_call | solution.py:53
  109.7 2.0 exponential_reduce_fusion.1
  112.3 1.9 fusion.42
  115.2 7.2 %shard_map.162 = bf16[4,128,192]{2,1,0:T(8,128)(2,1)} custom-call(bf16[4,128,192]{2,1,0:T(8,128)(2,1)} %copy.98.in_ref), custom_call_target="tpu_custom_call" | custom-call | tf_op jit(solution)/shard_map/pallas_call | solution.py:53
  126.5 7.5 %shard_map.163 = bf16[128,768]{1,0:T(8,128)(2,1)} custom-call(bf16[128,768]{1,0:T(8,128)(2,1)} %add_convert_fusion.3.in_ref), custom_call_target="tpu_custom_call" | custom-call | tf_op jit(solution)/shard_map/pallas_call | solution.py:53
  134.0 2.7 fusion.8
  136.7 3.3 fusion.10
  140.7 7.5 %shard_map.164 = bf16[128,768]{1,0:T(8,128)(2,1)} custom-call(bf16[128,768]{1,0:T(8,128)(2,1)} %slice.332.in_ref), custom_call_target="tpu_custom_call" | custom-call | tf_op jit(solution)/shard_map/pallas_call | solution.py:53
  149.6 2.7 convolution_convert_fusion.1
  154.9 13.7 %shard_map.165 = (bf16[4,128,192]{2,1,0:T(8,128)(2,1)}, bf16[8,128,384]{2,1,0:T(8,128)(2,1)}) custom-call(bf16[4,128,192]{2,1,0:T(8,128)(2,1)} %bitcast.321, bf16[4,128,384]{2,1,0:T(8,128)(2,1)} %pad_maximum_fusion.8.kv_ref), custom_call_target="tpu_custom_call" | custom-call | tf_op jit(solution)/shard_map/pallas_call | solution.py:53
  173.1 1.8 exponential_reduce_fusion
  175.8 1.9 fusion.43
  178.7 6.9 %shard_map.166 = bf16[4,128,192]{2,1,0:T(8,128)(2,1)} custom-call(bf16[4,128,192]{2,1,0:T(8,128)(2,1)} %copy.110.in_ref), custom_call_target="tpu_custom_call" | custom-call | tf_op jit(solution)/shard_map/pallas_call | solution.py:53
  190.6 9.1 %shard_map.167 = bf16[128,768]{1,0:T(8,128)(2,1)} custom-call(bf16[128,768]{1,0:T(8,128)(2,1)} %add_convert_fusion.2.in_ref), custom_call_target="tpu_custom_call" | custom-call | tf_op jit(solution)/shard_map/pallas_call | solution.py:53
  199.8 2.1 broadcast_select_fusion.9
  201.9 5.4 %broadcast_select_fusion.1 = (bf16[256,1536]{1,0:T(8,128)(2,1)}, bf16[256,1536]{1,0:T(8,128)(2,1)}, f32[256,1536]{1,0:T(8,128)}) fusion(pred[]{:T(512)S(6)} %eq.16, f32[256,1536]{1,0:T(8,128)} %copy-done.70, bf16[2,768,6272]{2,1,0:T(8,128)(2,1)} %bitcast.282, bf16[128,768]{1,0:T(8,128)(2,1)} %shard_map.167, bf16[128,768]{1,0:T(8,128)(2,1)} %add_convert_fusion.2.in_ref), kind=kOutput, calls=%fused_computation.103 | convolution fusion | flops 612630528 | bytes 7471105 | tf_op jit(solution)/shard_map/dot_general | solution.py:445
  207.9 9.1 %shard_map.169 = bf16[128,768]{1,0:T(8,128)(2,1)} custom-call(bf16[128,768]{1,0:T(8,128)(2,1)} %dynamic-slice_bitcast_fusion.in_ref), custom_call_target="tpu_custom_call" | custom-call | tf_op jit(solution)/shard_map/pallas_call | solution.py:53
  217.1 3.7 fusion.28
  220.8 2.7 fusion.11
  224.2 8.3 %shard_map.170 = bf16[128,768]{1,0:T(8,128)(2,1)} custom-call(bf16[128,768]{1,0:T(8,128)(2,1)} %slice.330.in_ref), custom_call_target="tpu_custom_call" | custom-call | tf_op jit(solution)/shard_map/pallas_call | solution.py:53
  236.5 2.6 convolution_convert_fusion.9
  242.7 6.9 %shard_map.171 = bf16[4,128,192]{2,1,0:T(8,128)(2,1)} custom-call(bf16[4,128,192]{2,1,0:T(8,128)(2,1)} %bitcast.324), custom_call_target="tpu_custom_call" | custom-call | tf_op jit(solution)/shard_map/pallas_call | solution.py:53
  253.0 4.8 convolution_convert_fusion.7
  257.9 2.6 multiply_reduce_fusion.1
  260.5 2.2 multiply_convert_fusion.1
  267.4 15.9 %shard_map.172 = (bf16[4,128,192]{2,1,0:T(8,128)(2,1)}, bf16[8,128,384]{2,1,0:T(8,128)(2,1)}) custom-call(bf16[4,128,192]{2,1,0:T(8,128)(2,1)} %copy.117.q_ref, bf16[8,128,384]{2,1,0:T(8,128)(2,1)} %pad_maximum_fusion.2.kv_ref), custom_call_target="tpu_custom_call" | custom-call | tf_op jit(solution)/shard_map/pallas_call | solution.py:53
  286.3 3.5 fusion.78
  291.1 7.5 %shard_map.173 = bf16[128,768]{1,0:T(8,128)(2,1)} custom-call(bf16[128,768]{1,0:T(8,128)(2,1)} %add_convert_fusion.1.in_ref), custom_call_target="tpu_custom_call" | custom-call | tf_op jit(solution)/shard_map/pallas_call | solution.py:53
  298.6 5.4 %broadcast_select_fusion.3 = (bf16[256,1536]{1,0:T(8,128)(2,1)}, bf16[256,1536]{1,0:T(8,128)(2,1)}, bf16[256,1536]{1,0:T(8,128)(2,1)S(1)}) fusion(bf16[256,1536]{1,0:T(8,128)(2,1)} %copy-done.71, pred[]{:T(512)S(6)} %eq.16, f32[256,1536]{1,0:T(8,128)} %copy-done.70, bf16[2,768,6272]{2,1,0:T(8,128)(2,1)} %bitcast.287, bf16[128,768]{1,0:T(8,128)(2,1)} %shard_map.173, ...), kind=kOutput, calls=%fused_computation.105 | convolution fusion | flops 613416960 | bytes 7471105 | tf_op jit(solution)/shard_map/dot_general | solution.py:445
  304.0 2.5 fusion.7
  307.2 7.5 %shard_map.174 = bf16[128,768]{1,0:T(8,128)(2,1)} custom-call(bf16[128,768]{1,0:T(8,128)(2,1)} %slice.329.in_ref), custom_call_target="tpu_custom_call" | custom-call | tf_op jit(solution)/shard_map/pallas_call | solution.py:53
  318.8 1.8 convolution_convert_fusion.8
  321.7 8.7 %shard_map.175 = bf16[4,128,192]{2,1,0:T(8,128)(2,1)} custom-call(bf16[4,128,192]{2,1,0:T(8,128)(2,1)} %bitcast.325), custom_call_target="tpu_custom_call" | custom-call | tf_op jit(solution)/shard_map/pallas_call | solution.py:53
  332.3 4.8 convolution_convert_fusion.6
  337.2 2.6 multiply_reduce_fusion
  339.8 1.8 multiply_convert_fusion
  346.4 15.6 %shard_map.176 = (bf16[4,128,192]{2,1,0:T(8,128)(2,1)}, bf16[8,128,384]{2,1,0:T(8,128)(2,1)}) custom-call(bf16[4,128,192]{2,1,0:T(8,128)(2,1)} %copy.126.q_ref, bf16[8,128,384]{2,1,0:T(8,128)(2,1)} %pad_maximum_fusion.3.kv_ref), custom_call_target="tpu_custom_call" | custom-call | tf_op jit(solution)/shard_map/pallas_call | solution.py:53
  364.8 3.5 fusion.72
  369.8 2.8 fusion.14
  373.6 9.1 %shard_map.168 = bf16[128,768]{1,0:T(8,128)(2,1)} custom-call(bf16[128,768]{1,0:T(8,128)(2,1)} %slice.331.in_ref), custom_call_target="tpu_custom_call" | custom-call | tf_op jit(solution)/shard_map/pallas_call | solution.py:53
  382.8 1.9 select_bitcast_fusion.1
  392.0 1.8 maximum_select_fusion.1
  396.3 2.8 pad_maximum_fusion.ga
  400.6 2.4 convolution_convert_fusion.4
  403.0 2.8 pad_maximum_fusion.1.gb
  405.8 101.3 %shard_map.177 = (f32[96,3072]{1,0:T(8,128)S(1)}, f32[96,3072]{1,0:T(8,128)S(1)}, f32[8,128]{1,0:T(8,128)S(1)}) custom-call(bf16[8,96,3072]{2,1,0:T(8,128)(2,1)} %pad_maximum_fusion.ga, bf16[8,96,3072]{2,1,0:T(8,128)(2,1)} %pad_maximum_fusion.1.gb, f32[8,8,128]{2,1,0:T(8,128)S(1)} %pad.9.gn), custom_call_target="tpu_custom_call" | custom-call | tf_op jit(solution)/shard_map/pallas_call | solution.py:53
  (342 shorter events, 91.0 us)
Async XLA Ops:
  0.7 6.1 %copy-start.48 = (bf16[1,1536,96]{1,2,0:T(8,128)(2,1)S(1)}, bf16[1,1536,96]{1,2,0:T(8,128)(2,1)}, u32[]{:S(2)}) copy-start(bf16[1,1536,96]{1,2,0:T(8,128)(2,1)} %param.15) | copy-start | bytes 884740
  1.8 366.6 %copy-start.65 = (f32[128]{0:T(128)}, f32[128]{0:T(128)S(1)}, u32[]{:S(2)}) copy-start(f32[128]{0:T(128)S(1)} %broadcast_multiply_fusion.3) | copy-start | bytes 1540
  2.9 365.5 %copy-start.67 = (f32[128]{0:T(128)}, f32[128]{0:T(128)S(1)}, u32[]{:S(2)}) copy-start(f32[128]{0:T(128)S(1)} %fusion.103) | copy-start | bytes 1540
  7.8 70.8 %copy-start.17 = (bf16[2,1,128,768]{3,2,1,0:T(8,128)(2,1)S(1)}, bf16[2,1,128,768]{3,2,1,0:T(8,128)(2,1)}, u32[]{:S(2)}) copy-start(bf16[2,1,128,768]{3,2,1,0:T(8,128)(2,1)} %param.9) | copy-start | bytes 1179652
  78.6 71.0 %copy-start.61 = (f32[768]{0:T(1024)}, f32[768]{0:T(1024)S(1)}, u32[]{:S(2)}) copy-start(f32[768]{0:T(1024)S(1)} %get-tuple-element.45) | copy-start | bytes 9220
  149.3 38.5 %copy-start.4 = (bf16[128,768]{1,0:T(8,128)(2,1)}, bf16[128,768]{1,0:T(8,128)(2,1)S(1)}, u32[]{:S(2)}) copy-start(bf16[128,768]{1,0:T(8,128)(2,1)S(1)} %get-tuple-element.62) | copy-start | bytes 589828
  149.3 140.8 %copy-start.63 = (f32[128]{0:T(128)}, f32[128]{0:T(128)S(1)}, u32[]{:S(2)}) copy-start(f32[128]{0:T(128)S(1)} %broadcast_multiply_fusion.1) | copy-start | bytes 1540
  149.5 140.6 %copy-start.64 = (f32[128]{0:T(128)}, f32[128]{0:T(128)S(1)}, u32[]{:S(2)}) copy-start(f32[128]{0:T(128)S(1)} %fusion.105) | copy-start | bytes 1540
  186.7 13.1 %copy-start.27 = (bf16[128,768]{1,0:T(8,128)(2,1)S(1)}, bf16[128,768]{1,0:T(8,128)(2,1)}, u32[]{:S(2)}) copy-start(bf16[128,768]{1,0:T(8,128)(2,1)} %add_convert_fusion.3.in_ref) | copy-start | bytes 589828
  186.7 13.1 %copy-start.42 = (bf16[128,768]{1,0:T(8,128)(2,1)S(1)}, bf16[128,768]{1,0:T(8,128)(2,1)}, u32[]{:S(2)}) copy-start(bf16[128,768]{1,0:T(8,128)(2,1)} %shard_map.163) | copy-start | bytes 589828
  187.6 201.8 %collective-permute-start.4 = (bf16[128,768]{1,0:T(8,128)(2,1)}, bf16[128,768]{1,0:T(8,128)(2,1)}, u32[]{:S(2)}, u32[]{:S(2)}) collective-permute-start(bf16[128,768]{1,0:T(8,128)(2,1)} %get-tuple-element.92), channel_id=1, source_target_pairs={{0,64},{64,0},{1,65},{65,1},{2,66},{66,2},{3,67},{67,3},{4,68},{68... | collective-permute-start | bytes 589832 | tf_op jit(solution)/shard_map/ppermute | solution.py:595
  201.9 5.4 %copy-start.32 = (bf16[2,1,128,768]{3,2,1,0:T(8,128)(2,1)S(1)}, bf16[2,1,128,768]{3,2,1,0:T(8,128)(2,1)}, u32[]{:S(2)}) copy-start(bf16[2,1,128,768]{3,2,1,0:T(8,128)(2,1)} %param.10) | copy-start | bytes 1179652
  201.9 198.7 %collective-permute-start.6 = (bf16[256,768]{1,0:T(8,128)(2,1)}, bf16[256,768]{1,0:T(8,128)(2,1)}, u32[]{:S(2)}, u32[]{:S(2)}) collective-permute-start(bf16[256,768]{1,0:T(8,128)(2,1)} %get-tuple-element.74), channel_id=1, source_target_pairs={{0,64},{64,0},{1,65},{65,1},{2,66},{66,2},{3,67},{67,3},{4,68},{68... | collective-permute-start | bytes 1179656 | tf_op jit(solution)/shard_map/ppermute | solution.py:595
  236.5 21.3 %slice-start.2 = ((s8[6291456]{0:T(1024)(128)(4,1)}), s8[2097152]{0:T(1024)(128)(4,1)S(1)}, s32[]{:S(2)}) async-start(s8[6291456]{0:T(1024)(128)(4,1)} %bitcast.273), calls=%async_computation.2 | async-start | bytes 4194304
  253.0 4.8 slice-start.3
  253.0 4.9 copy-start.31
  253.0 4.9 copy-start.44
  267.4 18.9 %copy-start.5 = (bf16[128,768]{1,0:T(8,128)(2,1)S(1)}, bf16[128,768]{1,0:T(8,128)(2,1)}, u32[]{:S(2)}) copy-start(bf16[128,768]{1,0:T(8,128)(2,1)} %copy-done.4) | copy-start | bytes 589828
  284.4 5.4 %copy-start.34 = (bf16[128,4,192]{0,2,1:T(8,128)(2,1)}, bf16[128,4,192]{0,2,1:T(8,128)(2,1)S(1)}, u32[]{:S(2)}) copy-start(bf16[128,4,192]{0,2,1:T(8,128)(2,1)S(1)} %copy.118) | copy-start | bytes 589828
  306.4 10.6 %copy-start.7 = (bf16[128,768]{1,0:T(8,128)(2,1)S(1)}, bf16[128,768]{1,0:T(8,128)(2,1)}, u32[]{:S(2)}) copy-start(bf16[128,768]{1,0:T(8,128)(2,1)} %add_convert_fusion.1.in_ref) | copy-start | bytes 589828
  306.5 10.6 %copy-start.26 = (bf16[128,768]{1,0:T(8,128)(2,1)S(1)}, bf16[128,768]{1,0:T(8,128)(2,1)}, u32[]{:S(2)}) copy-start(bf16[128,768]{1,0:T(8,128)(2,1)} %copy-done.25) | copy-start | bytes 589828
  317.1 13.3 %copy-start.66 = (f32[128]{0:T(128)}, f32[128]{0:T(128)S(1)}, u32[]{:S(2)}) copy-start(f32[128]{0:T(128)S(1)} %negate_multiply_fusion.1) | copy-start | bytes 1540
  318.7 71.0 %collective-permute-start.5 = (bf16[128,768]{1,0:T(8,128)(2,1)}, bf16[128,768]{1,0:T(8,128)(2,1)}, u32[]{:S(2)}, u32[]{:S(2)}) collective-permute-start(bf16[128,768]{1,0:T(8,128)(2,1)} %broadcast_select_fusion.10), channel_id=1, source_target_pairs={{0,64},{64,0},{1,65},{65,1},{2,66},{66,2},{3,67},{67,3},{4,68},{68... | collective-permute-start | bytes 589832 | tf_op jit(solution)/shard_map/ppermute | solution.py:595
  320.6 16.5 %slice-start = ((s8[6291456]{0:T(1024)(128)(4,1)}), s8[2097152]{0:T(1024)(128)(4,1)S(1)}, s32[]{:S(2)}) async-start(s8[6291456]{0:T(1024)(128)(4,1)} %bitcast.271), calls=%async_computation | async-start | bytes 4194304
  332.3 4.8 slice-start.1
  332.3 4.9 copy-start.29
  332.3 4.9 copy-start.45
  343.5 25.5 %copy-start.49 = (f32[1,768]{1,0:T(1,128)}, f32[1,768]{1,0:T(1,128)S(1)}, u32[]{:S(2)}) copy-start(f32[1,768]{1,0:T(1,128)S(1)} %reshape.552) | copy-start | bytes 9220
  343.5 25.5 %copy-start.51 = (f32[1,768]{1,0:T(1,128)}, f32[1,768]{1,0:T(1,128)S(1)}, u32[]{:S(2)}) copy-start(f32[1,768]{1,0:T(1,128)S(1)} %reshape.554) | copy-start | bytes 9220
  343.5 25.5 %copy-start.53 = (f32[1,768]{1,0:T(1,128)}, f32[1,768]{1,0:T(1,128)S(1)}, u32[]{:S(2)}) copy-start(f32[1,768]{1,0:T(1,128)S(1)} %reshape.549) | copy-start | bytes 9220
  343.5 25.4 %copy-start.55 = (f32[1,768]{1,0:T(1,128)}, f32[1,768]{1,0:T(1,128)S(1)}, u32[]{:S(2)}) copy-start(f32[1,768]{1,0:T(1,128)S(1)} %reshape.551) | copy-start | bytes 9220
  346.4 18.4 %copy-start.18 = (bf16[2,1,128,768]{3,2,1,0:T(8,128)(2,1)S(1)}, bf16[2,1,128,768]{3,2,1,0:T(8,128)(2,1)}, u32[]{:S(2)}) copy-start(bf16[2,1,128,768]{3,2,1,0:T(8,128)(2,1)} %param.9) | copy-start | bytes 1179652
  364.8 5.0 copy-start.72
  369.6 13.1 %copy-start.6 = (bf16[128,768]{1,0:T(8,128)(2,1)S(1)}, bf16[128,768]{1,0:T(8,128)(2,1)}, u32[]{:S(2)}) copy-start(bf16[128,768]{1,0:T(8,128)(2,1)} %copy-done.4) | copy-start | bytes 589828
  369.6 18.4 %collective-permute-start.10 = (f32[4,768]{1,0:T(4,128)}, f32[4,768]{1,0:T(4,128)}, u32[]{:S(2)}, u32[]{:S(2)}) collective-permute-start(f32[4,768]{1,0:T(4,128)} %broadcast_select_fusion.18), channel_id=1, source_target_pairs={{0,64},{64,0},{1,65},{65,1},{2,66},{66,2},{3,67},{67,3},{4,68},{68... | collective-permute-start | bytes 36872 | tf_op jit(solution)/shard_map/ppermute | solution.py:595
  372.6 12.1 %copy-start.8 = (bf16[128,768]{1,0:T(8,128)(2,1)S(1)}, bf16[128,768]{1,0:T(8,128)(2,1)}, u32[]{:S(2)}) copy-start(bf16[128,768]{1,0:T(8,128)(2,1)} %add_convert_fusion.1.in_ref) | copy-start | bytes 589828
  372.7 12.1 %copy-start.16 = (f32[128,768]{1,0:T(8,128)S(1)}, f32[128,768]{1,0:T(8,128)}, u32[]{:S(2)}) copy-start(f32[128,768]{1,0:T(8,128)} %copy-done.15) | copy-start | bytes 1179652
  382.7 4.0 copy-start.35
  382.7 4.0 copy-start.37
  386.8 5.0 collective-permute-start.1
  387.8 6.4 %copy-start.43 = (bf16[1,1,1,128,768]{4,3,2,1,0:T(8,128)(2,1)S(1)}, bf16[1,1,1,128,768]{4,3,2,1,0:T(8,128)(2,1)}, u32[]{:S(2)}) copy-start(bf16[1,1,1,128,768]{4,3,2,1,0:T(8,128)(2,1)} %get-tuple-element.59) | copy-start | bytes 589828
  388.0 7.2 %collective-permute-start.3 = (bf16[128,2304]{0,1:T(8,128)(2,1)}, bf16[128,2304]{0,1:T(8,128)(2,1)S(1)}, u32[]{:S(2)}, u32[]{:S(2)}) collective-permute-start(bf16[128,2304]{0,1:T(8,128)(2,1)} %get-tuple-element.72), channel_id=1, source_target_pairs={{0,64},{64,0},{1,65},{65,1},{2,66},{66,2},{3,67},{67,3},{4,68},{68... | collective-permute-start | bytes 1769480 | tf_op jit(solution)/shard_map/ppermute | solution.py:595
  389.4 5.6 %copy-start.69 = (bf16[256,1536]{1,0:T(8,128)(2,1)S(1)}, bf16[256,1536]{1,0:T(8,128)(2,1)}, u32[]{:S(2)}) copy-start(bf16[256,1536]{1,0:T(8,128)(2,1)} %get-tuple-element.68) | copy-start | bytes 2359300
  389.5 9.6 %collective-permute-start.9 = (bf16[256,1536]{1,0:T(8,128)(2,1)}, bf16[256,1536]{1,0:T(8,128)(2,1)S(1)}, u32[]{:S(2)}, u32[]{:S(2)}) collective-permute-start(bf16[256,1536]{1,0:T(8,128)(2,1)} %get-tuple-element.66), channel_id=1, source_target_pairs={{0,64},{64,0},{1,65},{65,1},{2,66},{66,2},{3,67},{67,3},{4,68},{68... | collective-permute-start | bytes 2359304 | tf_op jit(solution)/shard_map/ppermute | solution.py:595
  389.6 4.2 collective-permute-start
  391.8 3.2 collective-permute-start.2
  393.8 5.3 %collective-permute-start.8 = (bf16[256,768]{1,0:T(8,128)(2,1)S(1)}, bf16[256,768]{1,0:T(8,128)(2,1)S(1)}, u32[]{:S(2)}, u32[]{:S(2)}) collective-permute-start(bf16[256,768]{1,0:T(8,128)(2,1)S(1)} %get-tuple-element.76), channel_id=1, source_target_pairs={{0,64},{64,0},{1,65},{65,1},{2,66},{66,2},{3,67},{67,3},{4,68},{68... | collective-permute-start | bytes 1179656 | tf_op jit(solution)/shard_map/ppermute | solution.py:595
  395.1 5.5 %collective-permute-start.7 = (bf16[256,1536]{1,0:T(8,128)(2,1)S(1)}, bf16[256,1536]{1,0:T(8,128)(2,1)S(1)}, u32[]{:S(2)}, u32[]{:S(2)}) collective-permute-start(bf16[256,1536]{1,0:T(8,128)(2,1)S(1)} %copy-done.69), channel_id=1, source_target_pairs={{0,64},{64,0},{1,65},{65,1},{2,66},{66,2},{3,67},{67,3},{4,68},{68... | collective-permute-start | bytes 2359304 | tf_op jit(solution)/shard_map/ppermute | solution.py:595
  (42 other events, 106.4 us)

commit v2 on v1

--- a/solution.py
+++ b/solution.py
@@ -184,80 +184,6 @@
     return context, tensor, span, peers
 
 
-def heads_body(by_span, q_ref, kv_ref, q_out, kv_out, send_sems, recv_sems, local_sems):
-    context, tensor, span, peers = span_peers()
-    greet([{"context": c, "tensor": t} for _, c, t in peers])
-    copies = Copies(send_sems, recv_sems)
-    for peer, c, t in peers:
-        copies.push(
-            kv_ref.at[peer if by_span else c], kv_out.at[span], {"context": c, "tensor": t}
-        )
-    for step in range(1, 4):
-        c = lax.rem(context + step, 4)
-        copies.push(q_ref.at[c], q_out.at[context], {"context": c})
-    own = [
-        pltpu.make_async_copy(q_ref.at[context], q_out.at[context], local_sems.at[0]),
-        pltpu.make_async_copy(
-            kv_ref.at[span if by_span else context], kv_out.at[span], local_sems.at[1]
-        ),
-    ]
-    for copy in own:
-        copy.start()
-    for copy in copies.made:
-        copy.wait_recv()
-    copies.finish()
-    for copy in own:
-        copy.wait()
-
-
-def exchange_heads(q_parts, kv_parts, by_span):
-    return call_remote(
-        functools.partial(heads_body, by_span),
-        (
-            jax.ShapeDtypeStruct(q_parts.shape, q_parts.dtype),
-            jax.ShapeDtypeStruct((8, *kv_parts.shape[1:]), kv_parts.dtype),
-        ),
-        10,
-        1 if by_span else 2,
-        (q_parts, kv_parts),
-        locals_=2,
-    )
-
-
-def context_body(in_ref, out_ref, send_sems, recv_sems, local_sems):
-    context = lax.axis_index("context")
-    peers = [lax.rem(context + step, 4) for step in range(1, 4)]
-    greet([{"context": c} for c in peers])
-    copies = Copies(send_sems, recv_sems)
-    for c in peers:
-        copies.push(in_ref.at[c], out_ref.at[context], {"context": c})
-    own = pltpu.make_async_copy(in_ref.at[context], out_ref.at[context], local_sems.at[0])
-    own.start()
-    for copy in copies.made:
-        copy.wait_recv()
-    copies.finish()
-    own.wait()
-
-
-def exchange_context(parts):
-    return call_remote(
-        context_body, jax.ShapeDtypeStruct(parts.shape, parts.dtype), 3, 3, (parts,)
-    )
-
-
-def pair_body(in_ref, out_ref, send_sems, recv_sems, local_sems):
-    peer = {"tensor": 1 - lax.axis_index("tensor")}
-    greet([peer])
-    copies = Copies(send_sems, recv_sems)
-    copies.push(in_ref, out_ref, peer)
-    copies.made[0].wait_recv()
-    copies.finish()
-
-
-def exchange_pair(rows):
-    return call_remote(pair_body, jax.ShapeDtypeStruct(rows.shape, rows.dtype), 1, 4, (rows,))
-
-
 BLOCK = 16
 
 
@@ -430,15 +356,16 @@
     )
 
 
-def layer_norm(values, gain_vec, bias_vec):
-    row_mean = jnp.mean(values, -1, keepdims=True)
-    centred = values - row_mean
-    variance = jnp.mean(centred * centred, -1, keepdims=True)
-    return centred * lax.rsqrt(variance + EPSILON) * gain_vec + bias_vec
-
-
-def smooth_unit(values):
-    return jax.nn.gelu(values, approximate=True)
+TOKENS = 128
+SPANS = 8
+GROUPS = 4
+GROUP_HEADS = 3
+WIDTH = 768
+PAIR = 2 * HEAD_DIM
+KV_GROUP = GROUP_HEADS * PAIR
+SCALE = 1.0 / math.sqrt(HEAD_DIM)
+GELU_A = math.sqrt(2.0 / math.pi)
+GELU_B = 0.044715
 
 
 def dot(first, second):
@@ -453,16 +380,435 @@
     return lax.dot_general(first, second, (((1,), (1,)), ((), ())), preferred_element_type=F32)
 
 
-def to_groups(rows):
-    return rows.reshape(rows.shape[0], 4, -1).transpose(1, 0, 2)
-
-
-def from_groups(groups):
-    return groups.transpose(1, 0, 2).reshape(groups.shape[1], -1)
-
-
-def heads_of(rows):
-    return rows.reshape(rows.shape[0], -1, HEAD_DIM)
+def normalised(values):
+    centred = values - jnp.mean(values, -1, keepdims=True)
+    inverse = lax.rsqrt(jnp.mean(centred * centred, -1, keepdims=True) + EPSILON)
+    return centred * inverse, inverse
+
+
+def norm_pull(values, gain, grad):
+    unit, inverse = normalised(values)
+    scaled = grad * gain
+    along = jnp.mean(scaled * unit, -1, keepdims=True)
+    pulled = inverse * (scaled - jnp.mean(scaled, -1, keepdims=True) - unit * along)
+    return pulled, jnp.sum(grad * unit, 0, keepdims=True), jnp.sum(grad, 0, keepdims=True)
+
+
+def gelu(u):
+    return 0.5 * u * (1.0 + jnp.tanh(GELU_A * (u + GELU_B * u * u * u)))
+
+
+def gelu_slope(u):
+    tanh = jnp.tanh(GELU_A * (u + GELU_B * u * u * u))
+    rise = GELU_A * (1.0 + 3.0 * GELU_B * u * u)
+    return 0.5 * (1.0 + tanh) + 0.5 * u * (1.0 - tanh * tanh) * rise
+
+
+def lower_lanes(rows):
+    return lax.broadcasted_iota(jnp.int32, (rows, PAIR), 1) < HEAD_DIM
+
+
+def swapped(value):
+    return pltpu.roll(value, HEAD_DIM, 1)
+
+
+def split_groups(value):
+    low = lower_lanes(value.shape[0])
+    groups = []
+    for base in (0, 384):
+        t0, t1, t2 = (value[:, base + 128 * k : base + 128 * (k + 1)] for k in range(3))
+        s1, s2 = swapped(t1), swapped(t2)
+        groups.append(jnp.concatenate([t0, jnp.where(low, t1, 0.0)], 1))
+        groups.append(jnp.concatenate([jnp.where(low, s1, s2), jnp.where(low, s2, 0.0)], 1))
+    return groups
+
+
+def join_groups(groups):
+    low = lower_lanes(groups[0].shape[0])
+    parts = []
+    for first, second in ((groups[0], groups[1]), (groups[2], groups[3])):
+        a0, b0, a1, b1 = first[:, :128], first[:, 128:], second[:, :128], second[:, 128:]
+        s1 = swapped(a1)
+        parts += [a0, jnp.where(low, b0, s1), jnp.where(low, s1, swapped(b1))]
+    return jnp.concatenate(parts, 1)
+
+
+def head_columns(group, at_upper):
+    low = lower_lanes(group.shape[0])
+    first, last = group[:, :128], group[:, 128:]
+    if at_upper:
+        return [
+            jnp.where(low, 0.0, swapped(first)),
+            jnp.where(low, 0.0, first),
+            jnp.where(low, 0.0, swapped(last)),
+        ]
+    return [jnp.where(low, first, 0.0), jnp.where(low, swapped(first), 0.0), jnp.where(low, last, 0.0)]
+
+
+class Links:
+    def __init__(self, send_sems, recv_sems):
+        self.send_sems, self.recv_sems, self.sent, self.count = send_sems, recv_sems, [], 0
+
+    def copy(self, src, dst, recv_index, device_id):
+        made = pltpu.make_async_remote_copy(
+            src_ref=src,
+            dst_ref=dst,
+            send_sem=self.send_sems.at[self.count],
+            recv_sem=self.recv_sems.at[recv_index],
+            device_id=device_id,
+            device_id_type=MESH,
+        )
+        self.count += 1
+        return made
+
+    def push(self, src, dst, recv_index, device_id, unless=None):
+        made = self.copy(src, dst, recv_index, device_id)
+        if unless is None:
+            made.start()
+        else:
+            pl.when(jnp.logical_not(unless))(made.start)
+        self.sent.append((made, unless))
+
+    def arrived(self, dst, recv_index, unless=None):
+        made = pltpu.make_async_remote_copy(
+            src_ref=dst,
+            dst_ref=dst,
+            send_sem=self.send_sems.at[0],
+            recv_sem=self.recv_sems.at[recv_index],
+            device_id={"tensor": 1 - lax.axis_index("tensor")},
+            device_id_type=MESH,
+        )
+        if unless is None:
+            made.wait_recv()
+        else:
+            pl.when(jnp.logical_not(unless))(made.wait_recv)
+
+    def finish(self):
+        for made, unless in self.sent:
+            if unless is None:
+                made.wait_send()
+            else:
+                pl.when(jnp.logical_not(unless))(made.wait_send)
+
+
+KV_AT, Q_AT, O_AT, PAIR_AT = 0, 8, 12, 16
+UNITS = 1536
+COLUMNS = (("q", 0, 3 * WIDTH), ("o", 3 * WIDTH, WIDTH), ("f", 4 * WIDTH, UNITS), ("p", 4 * WIDTH + UNITS, UNITS))
+
+
+def load_weights(block, w_ref, buffers, sems):
+    loads = []
+    for index, ((_, start, size), buffer) in enumerate(zip(COLUMNS, buffers)):
+        load = pltpu.make_async_copy(w_ref.at[block, :, pl.ds(start, size)], buffer, sems.at[index])
+        load.start()
+        loads.append(load)
+    return loads
+
+
+def allowed_keys(quarter, tensor, seg_keys, seg_queries):
+    keys = 256 * (quarter + 1)
+    rows = (2 * quarter + tensor) * TOKENS + lax.broadcasted_iota(jnp.int32, (TOKENS, keys), 0)
+    columns = lax.broadcasted_iota(jnp.int32, (TOKENS, keys), 1)
+    same = seg_keys[:, :keys] == seg_queries[quarter * TOKENS : (quarter + 1) * TOKENS, :]
+    return (columns <= rows) & same
+
+
+def head_rows(kv_all, quarter, head):
+    spans = 2 * (quarter + 1)
+    rows = kv_all[0:spans, :, head * PAIR : (head + 1) * PAIR]
+    return rows.reshape(spans * TOKENS, PAIR)
+
+
+def tiles(total, tile, body):
+    def step(index, _):
+        body(pl.ds(pl.multiple_of(index * tile, tile), tile))
+        return 0
+
+    lax.fori_loop(0, total // tile, step, 0)
+
+
+def forward_body(
+    block, x_ref, segk_ref, segq_ref, norms_ref, w_ref,
+    y_out, a_out, q_out, kv_out, lse_out, mixed_out, resid_out, inner_out, up_out, act_out,
+    wq, wo, wf, wp, kvb, kv_all, qb, q_all, ob, o_all, inner, down, down_in,
+    send_sems, recv_sems, local_sems,
+):
+    context, tensor, span, spans = span_peers()
+    greet([{"context": c, "tensor": t} for _, c, t in spans])
+    loads = load_weights(block, w_ref, (wq, wo, wf, wp), local_sems)
+    links = Links(send_sems, recv_sems)
+    peer = {"tensor": 1 - tensor}
+
+    x = x_ref[...].astype(F32)
+    unit, _ = normalised(x)
+    a_out[...] = (unit * norms_ref[0:1, :] + norms_ref[2:3, :]).astype(BF16)
+    loads[0].wait()
+    for step in range(1, 5):
+        group = lax.rem(context + step, 4)
+        columns = pl.ds(pl.multiple_of(WIDTH + group * KV_GROUP, 128), KV_GROUP)
+        kvb[group] = dot(a_out[...], wq[:, columns]).astype(BF16)
+        links.push(kvb.at[group], kv_all.at[span], KV_AT + span, {"context": group, "tensor": 1 - tensor})
+        if step < 4:
+            links.push(kvb.at[group], kv_all.at[span], KV_AT + span, {"context": group})
+        else:
+            kv_all[span] = kvb[group]
+    for index, part in enumerate(split_groups(dot(a_out[...], wq[:, :WIDTH]))):
+        qb[index] = part.astype(BF16)
+    for step in range(1, 4):
+        group = lax.rem(context + step, 4)
+        links.push(qb.at[group], q_all.at[context], Q_AT + context, {"context": group})
+    q_all[context] = qb[context]
+
+    for quarter in range(GROUPS):
+        for index in (2 * quarter, 2 * quarter + 1):
+            links.arrived(kv_all.at[index], KV_AT + index, index == span)
+        links.arrived(q_all.at[quarter], Q_AT + quarter, quarter == context)
+        allowed = allowed_keys(quarter, tensor, segk_ref, segq_ref)
+        queries = head_columns(q_all[quarter].astype(F32) * SCALE, False)
+        low = lower_lanes(TOKENS)
+        outs = []
+        for head in range(GROUP_HEADS):
+            rows = head_rows(kv_all, quarter, head)
+            masked = jnp.where(allowed, dot_nt(queries[head].astype(BF16), rows), MASKED)
+            top = jnp.max(masked, -1, keepdims=True)
+            weight = jnp.exp(masked - top)
+            total = jnp.sum(weight, -1, keepdims=True)
+            lse_out[quarter * GROUP_HEADS + head] = top + jnp.log(total)
+            outs.append(dot(weight.astype(BF16), rows) * (1.0 / total))
+        pair = jnp.where(low, swapped(outs[0]), outs[1])
+        last = jnp.where(low, swapped(outs[2]), 0.0)
+        ob[quarter] = jnp.concatenate([pair, last], 1).astype(BF16)
+        links.push(ob.at[quarter], o_all.at[context], O_AT + context, {"context": quarter}, quarter == context)
+    o_all[context] = ob[context]
+    q_out[...] = q_all[...]
+    kv_out[...] = kv_all[...]
+    for index in range(GROUPS):
+        links.arrived(o_all.at[index], O_AT + index, index == context)
+    mixed_out[...] = join_groups([o_all[index].astype(F32) for index in range(GROUPS)]).astype(BF16)
+    loads[1].wait()
+    resid = x + dot(mixed_out[...], wo[...])
+    resid_out[...] = resid
+    unit, _ = normalised(resid)
+    inner[0] = (unit * norms_ref[1:2, :] + norms_ref[3:4, :]).astype(BF16)
+    links.push(inner.at[0], inner.at[1], PAIR_AT, peer)
+    loads[2].wait()
+    loads[3].wait()
+
+    def upward(half):
+        rows = pl.ds(half * TOKENS, TOKENS)
+
+        def tile(columns):
+            up = dot(inner[half], wf[:, columns])
+            up_out[rows, columns] = up
+            act_out[rows, columns] = gelu(up).astype(BF16)
+
+        tiles(UNITS, 512, tile)
+
+    upward(0)
+    links.arrived(inner.at[1], PAIR_AT)
+    upward(1)
+
+    def down_tile(half, columns):
+        return dot_nt(act_out[half * TOKENS : (half + 1) * TOKENS, :], wp[columns, :])
+
+    def down_peer(columns):
+        down[:, columns] = down_tile(1, columns).astype(BF16)
+
+    tiles(WIDTH, 256, down_peer)
+    links.push(down, down_in, PAIR_AT + 1, peer)
+    inner_out[0:TOKENS, :] = inner[0]
+    inner_out[TOKENS:, :] = inner[1]
+    own = resid_out[...] + down_tile(0, slice(None))
+    links.arrived(down_in, PAIR_AT + 1)
+    y_out[...] = (own + down_in[...].astype(F32)).astype(BF16)
+    links.finish()
+
+
+def shape(dims, kind=BF16):
+    return jax.ShapeDtypeStruct(dims, kind)
+
+
+def weight_buffers():
+    return [pltpu.VMEM((WIDTH, size), BF16) for _, _, size in COLUMNS]
+
+
+def forward_block(block, x, seg_keys, seg_queries, norms, full):
+    return call_remote(
+        functools.partial(forward_body, block),
+        (
+            shape((TOKENS, WIDTH)),
+            shape((TOKENS, WIDTH)),
+            shape((GROUPS, TOKENS, 256)),
+            shape((SPANS, TOKENS, KV_GROUP)),
+            shape((GROUPS * GROUP_HEADS, TOKENS, 1), F32),
+            shape((TOKENS, WIDTH)),
+            shape((TOKENS, WIDTH), F32),
+            shape((2 * TOKENS, WIDTH)),
+            shape((2 * TOKENS, UNITS), F32),
+            shape((2 * TOKENS, UNITS)),
+        ),
+        20,
+        6 + block,
+        (x, seg_keys, seg_queries, norms, full),
+        scratch=[
+            *weight_buffers(),
+            pltpu.VMEM((GROUPS, TOKENS, KV_GROUP), BF16),
+            pltpu.VMEM((SPANS, TOKENS, KV_GROUP), BF16),
+            pltpu.VMEM((GROUPS, TOKENS, 256), BF16),
+            pltpu.VMEM((GROUPS, TOKENS, 256), BF16),
+            pltpu.VMEM((GROUPS, TOKENS, 256), BF16),
+            pltpu.VMEM((GROUPS, TOKENS, 256), BF16),
+            pltpu.VMEM((2, TOKENS, WIDTH), BF16),
+            pltpu.VMEM((TOKENS, WIDTH), BF16),
+            pltpu.VMEM((TOKENS, WIDTH), BF16),
+        ],
+        locals_=4,
+        specs=([VMEM] * 4 + [ANY], (VMEM,) * 10),
+        vmem=48 * 1024 * 1024,
+    )
+
+
+def backward_body(
+    block, dy_ref, x_ref, q_ref, kv_ref, lse_ref, resid_ref, up_ref, segk_ref, segq_ref, norms_ref, w_ref,
+    dx_out, dqkv_out, low_out, dyall_out, du_out, vec_out,
+    wq, wo, wf, wp, dyall, down, down_in, dob, do_all, dqb, dq_all, dkv_sum, dkvb, dkv_all,
+    send_sems, recv_sems, local_sems,
+):
+    context, tensor, span, spans = span_peers()
+    greet([{"context": c, "tensor": t} for _, c, t in spans])
+    links = Links(send_sems, recv_sems)
+    peer = {"tensor": 1 - tensor}
+    dyall[0] = dy_ref[...]
+    links.push(dyall.at[0], dyall.at[1], PAIR_AT, peer)
+    loads = load_weights(block, w_ref, (wq, wo, wf, wp), local_sems)
+    loads[3].wait()
+
+    def upward(half):
+        rows = pl.ds(half * TOKENS, TOKENS)
+
+        def tile(columns):
+            grad = dot(dyall[half], wp[:, columns])
+            du_out[rows, columns] = (grad * gelu_slope(up_ref[rows, columns])).astype(BF16)
+
+        tiles(UNITS, 512, tile)
+
+    def inner_grad(half, columns):
+        return dot_nt(du_out[half * TOKENS : (half + 1) * TOKENS, :], wf[columns, :])
+
+    def down_peer(columns):
+        down[:, columns] = inner_grad(1, columns).astype(BF16)
+
+    upward(0)
+    links.arrived(dyall.at[1], PAIR_AT)
+    upward(1)
+    loads[2].wait()
+    tiles(WIDTH, 256, down_peer)
+    links.push(down, down_in, PAIR_AT + 1, peer)
+    own = inner_grad(0, slice(None))
+    dyall_out[0:TOKENS, :] = dyall[0]
+    dyall_out[TOKENS:, :] = dyall[1]
+    links.arrived(down_in, PAIR_AT + 1)
+    inner = own + down_in[...].astype(F32)
+    pulled, gain_late, bias_late = norm_pull(resid_ref[...], norms_ref[1:2, :], inner)
+    resid_grad = dy_ref[...].astype(F32) + pulled
+    low_out[...] = resid_grad.astype(BF16)
+    loads[1].wait()
+    for index, part in enumerate(split_groups(dot_nt(low_out[...], wo[...]))):
+        dob[index] = part.astype(BF16)
+    for step in range(1, 4):
+        group = lax.rem(context + step, 4)
+        links.push(dob.at[group], do_all.at[context], O_AT + context, {"context": group})
+    do_all[context] = dob[context]
+
+    low = lower_lanes(TOKENS)
+    for quarter in reversed(range(GROUPS)):
+        links.arrived(do_all.at[quarter], O_AT + quarter, quarter == context)
+        allowed = allowed_keys(quarter, tensor, segk_ref, segq_ref)
+        queries = head_columns(q_ref[quarter].astype(F32) * SCALE, False)
+        grads = head_columns(do_all[quarter].astype(F32), True)
+        outs = []
+        count = 2 * (quarter + 1)
+        for head in range(GROUP_HEADS):
+            rows = head_rows(kv_ref, quarter, head)
+            query, grad = queries[head].astype(BF16), grads[head].astype(BF16)
+            masked = jnp.where(allowed, dot_nt(query, rows), MASKED)
+            probs = jnp.exp(masked - lse_ref[quarter * GROUP_HEADS + head])
+            prob_grad = dot_nt(grad, rows)
+            centre = jnp.sum(probs * prob_grad, -1, keepdims=True)
+            score_grad = (probs * (prob_grad - centre)).astype(BF16)
+            outs.append(dot(score_grad, rows) * SCALE)
+            part = dot_tn(score_grad, query) + dot_tn(probs.astype(BF16), grad)
+            part = part.reshape(count, TOKENS, PAIR)
+            at = slice(head * PAIR, (head + 1) * PAIR)
+            if quarter == GROUPS - 1:
+                dkv_sum[0:count, :, at] = part
+            else:
+                dkv_sum[0:count, :, at] += part
+        pair = jnp.where(low, outs[0], swapped(outs[1]))
+        last = jnp.where(low, outs[2], 0.0)
+        dqb[quarter] = jnp.concatenate([pair, last], 1).astype(BF16)
+        links.push(dqb.at[quarter], dq_all.at[context], Q_AT + context, {"context": quarter}, quarter == context)
+        for index in (2 * quarter, 2 * quarter + 1):
+            dkvb[index] = dkv_sum[index].astype(BF16)
+            links.push(
+                dkvb.at[index], dkv_all.at[span], KV_AT + span,
+                {"context": quarter, "tensor": index - 2 * quarter}, index == span,
+            )
+    dq_all[context] = dqb[context]
+    dkv_all[span] = dkvb[span]
+    for index in range(GROUPS):
+        links.arrived(dq_all.at[index], Q_AT + index, index == context)
+    joined = join_groups([dq_all[index].astype(F32) for index in range(GROUPS)])
+    dqkv_out[:, :WIDTH] = joined.astype(BF16)
+    for index in range(SPANS):
+        links.arrived(dkv_all.at[index], KV_AT + index, index == span)
+    for group in range(GROUPS):
+        total = dkv_all[2 * group].astype(F32) + dkv_all[2 * group + 1].astype(F32)
+        at = WIDTH + group * KV_GROUP
+        dqkv_out[:, at : at + KV_GROUP] = total.astype(BF16)
+    loads[0].wait()
+    normed_grad = dot_nt(dqkv_out[...], wq[...])
+    pulled, gain_early, bias_early = norm_pull(x_ref[...].astype(F32), norms_ref[0:1, :], normed_grad)
+    dx_out[...] = (resid_grad + pulled).astype(BF16)
+    vec_out[0:1, :] = gain_early
+    vec_out[1:2, :] = gain_late
+    vec_out[2:3, :] = bias_early
+    vec_out[3:4, :] = bias_late
+    vec_out[4:8, :] = jnp.zeros((4, WIDTH), F32)
+    links.finish()
+
+
+def backward_block(block, dy, x, q_all, kv_all, lse, resid, up, seg_keys, seg_queries, norms, full):
+    return call_remote(
+        functools.partial(backward_body, block),
+        (
+            shape((TOKENS, WIDTH)),
+            shape((TOKENS, 3 * WIDTH)),
+            shape((TOKENS, WIDTH)),
+            shape((2 * TOKENS, WIDTH)),
+            shape((2 * TOKENS, UNITS)),
+            shape((8, WIDTH), F32),
+        ),
+        20,
+        8 + block,
+        (dy, x, q_all, kv_all, lse, resid, up, seg_keys, seg_queries, norms, full),
+        scratch=[
+            *weight_buffers(),
+            pltpu.VMEM((2, TOKENS, WIDTH), BF16),
+            pltpu.VMEM((TOKENS, WIDTH), BF16),
+            pltpu.VMEM((TOKENS, WIDTH), BF16),
+            pltpu.VMEM((GROUPS, TOKENS, 256), BF16),
+            pltpu.VMEM((GROUPS, TOKENS, 256), BF16),
+            pltpu.VMEM((GROUPS, TOKENS, 256), BF16),
+            pltpu.VMEM((GROUPS, TOKENS, 256), BF16),
+            pltpu.VMEM((SPANS, TOKENS, KV_GROUP), F32),
+            pltpu.VMEM((SPANS, TOKENS, KV_GROUP), BF16),
+            pltpu.VMEM((SPANS, TOKENS, KV_GROUP), BF16),
+        ],
+        locals_=4,
+        specs=([VMEM] * 10 + [ANY], (VMEM,) * 6),
+        vmem=48 * 1024 * 1024,
+    )
 
 
 def per_device(
@@ -473,121 +819,50 @@
     tokens, width = block_input.shape[2:]
     units = w_fc.shape[2]
     depth = w_qkv.shape[1]
-    group = width // 4
-    scale = 1.0 / math.sqrt(HEAD_DIM)
-
+    heads = width // HEAD_DIM
+
+    pairs = w_qkv[0][:, width:].reshape(depth, 2, heads, HEAD_DIM).transpose(0, 2, 1, 3)
     vectors = jnp.concatenate([norm_gains[0], norm_biases[0]], 0)
     vectors = jnp.pad(vectors.T, ((0, 0), (0, 124)))
-    own = jnp.concatenate([w_qkv[0], w_out[0], w_fc[0], w_proj[0].T, vectors], 1)
+    own = jnp.concatenate(
+        [
+            w_qkv[0][:, :width],
+            pairs.reshape(depth, 2 * width),
+            w_out[0],
+            w_fc[0],
+            w_proj[0].T,
+            vectors,
+        ],
+        1,
+    )
     full = gather_weights(own).reshape(2, width, -1)
-
-    def weights(block):
-        edges = [0, 3 * width, 4 * width, 4 * width + units, 4 * width + 2 * units]
-        pieces = [full[block, :, edges[k] : edges[k + 1]] for k in range(4)]
-        norms = full[block, :, edges[4] : edges[4] + 4].T.astype(F32)
-        return (*pieces, norms)
+    norms = full[:, :, 4 * width + 2 * units : 4 * width + 2 * units + 8].transpose(0, 2, 1).astype(F32)
 
     def mine(stacked):
         return lax.dynamic_index_in_dim(stacked, section, 0, keepdims=False)
 
-    seg_keys = mine(segment_ids)[0]
+    seg_keys = mine(segment_ids)
     seg_queries = lax.dynamic_index_in_dim(
         seg_keys.reshape(4, 2, tokens), tensor, 1, keepdims=False
-    ).reshape(-1)
-    key_pos = jnp.arange(8 * tokens)
-    query_pos = lax.dynamic_index_in_dim(
-        key_pos.reshape(4, 2, tokens), tensor, 1, keepdims=False
-    ).reshape(-1)
-    allowed = (key_pos[None, :] <= query_pos[:, None]) & (
-        seg_keys[None, :] == seg_queries[:, None]
-    )
-
-    def masked_scores(query, keys):
-        raw = jnp.einsum("qhd,khd->hqk", query, keys, preferred_element_type=F32)
-        return jnp.where(allowed[None], raw * scale, MASKED)
+    ).reshape(-1, 1)
 
     def forward(block, entry):
-        qkv, out, fc, proj, norms = weights(block)
-        inputs = entry.astype(F32)
-        normed = layer_norm(inputs, norms[0], norms[2]).astype(BF16)
-        projected = dot(normed, qkv).astype(BF16)
-        q_parts = to_groups(projected[:, :width])
-        kv_parts = jnp.concatenate(
-            [to_groups(projected[:, width : 2 * width]), to_groups(projected[:, 2 * width :])], 2
+        sent, normed, q_all, kv_all, lse, mixed, resid, inner, up, act = forward_block(
+            block, entry, seg_keys, seg_queries, norms[block], full
         )
-        q_all, kv_all = exchange_heads(q_parts, kv_parts, False)
-        query = heads_of(q_all.reshape(-1, group))
-        kv_all = kv_all.reshape(-1, 2 * group)
-        keys, values = heads_of(kv_all[:, :group]), heads_of(kv_all[:, group:])
-        masked = masked_scores(query, keys)
-        totals = jax.nn.logsumexp(masked, axis=-1)
-        probs_low = jnp.exp(masked - totals[..., None]).astype(BF16)
-        mixed = jnp.einsum("hqk,khd->qhd", probs_low, values, preferred_element_type=F32)
-        mixed = mixed.reshape(4, tokens, group).astype(BF16)
-        mixed = from_groups(exchange_context(mixed))
-        resid = inputs + dot(mixed, out)
-        inner = layer_norm(resid, norms[1], norms[3]).astype(BF16)
-        inner_all = jnp.concatenate([inner, exchange_pair(inner)], 0)
-        upward = dot(inner_all, fc)
-        active = smooth_unit(upward).astype(BF16)
-        down = dot_nt(active, proj)
-        down = down[:tokens] + exchange_pair(down[tokens:].astype(BF16)).astype(F32)
-        sent = (resid + down).astype(BF16)
-        return sent, (entry, normed, query, keys, values, totals, mixed, resid, inner_all, upward, active)
-
-    def backward(block, incoming, kept):
-        qkv, out, fc, proj, norms = weights(block)
-        entry, normed, query, keys, values, totals, mixed, resid, inner_all, upward, active = kept
-        incoming_all = jnp.concatenate([incoming, exchange_pair(incoming)], 0)
-        active_grad = dot(incoming_all, proj)
-        _, unit_pull = jax.vjp(smooth_unit, upward)
-        upward_grad = unit_pull(active_grad)[0].astype(BF16)
-        inner_grad = dot_nt(upward_grad, fc)
-        inner_grad = inner_grad[:tokens] + exchange_pair(inner_grad[tokens:].astype(BF16)).astype(F32)
-        _, late_pull = jax.vjp(layer_norm, resid, norms[1], norms[3])
-        resid_part, gain_late, bias_late = late_pull(inner_grad)
-        resid_grad = incoming.astype(F32) + resid_part
-        resid_low = resid_grad.astype(BF16)
-        mixed_grad = dot_nt(resid_low, out).astype(BF16)
-        mixed_heads = heads_of(exchange_context(to_groups(mixed_grad)).reshape(-1, group))
-        probs = jnp.exp(masked_scores(query, keys) - totals[..., None])
-        probs_low = probs.astype(BF16)
-        prob_grad = jnp.einsum("qhd,khd->hqk", mixed_heads, values, preferred_element_type=F32)
-        centre = jnp.sum(probs * prob_grad, -1, keepdims=True)
-        score_grad = (probs * (prob_grad - centre)).astype(BF16)
-        q_grad = jnp.einsum("hqk,khd->qhd", score_grad, keys, preferred_element_type=F32) * scale
-        k_grad = jnp.einsum("hqk,qhd->khd", score_grad, query, preferred_element_type=F32) * scale
-        v_grad = jnp.einsum("hqk,qhd->khd", probs_low, mixed_heads, preferred_element_type=F32)
-        kv_grad = jnp.concatenate(
-            [k_grad.reshape(8, tokens, group), v_grad.reshape(8, tokens, group)], 2
+        return sent, (entry, q_all, kv_all, lse, resid, up), (normed, mixed, inner, act)
+
+    def backward(block, incoming, kept, operands):
+        sent, projected, low, incoming_all, up_grad, vectors = backward_block(
+            block, incoming, *kept, seg_keys, seg_queries, norms[block], full
         )
-        q_back, kv_back = exchange_heads(
-            q_grad.reshape(4, tokens, group).astype(BF16), kv_grad.astype(BF16), True
-        )
-        kv_back = jnp.sum(kv_back.reshape(4, 2, tokens, 2 * group).astype(F32), 1).astype(BF16)
-        projected_grad = jnp.concatenate(
-            [
-                from_groups(q_back),
-                from_groups(kv_back[:, :, :group]),
-                from_groups(kv_back[:, :, group:]),
-            ],
-            1,
-        )
-        normed_grad = dot_nt(projected_grad, qkv)
-        _, early_pull = jax.vjp(layer_norm, entry.astype(F32), norms[0], norms[2])
-        input_part, gain_early, bias_early = early_pull(normed_grad)
-        sent_grad = (resid_grad + input_part).astype(BF16)
-        vector_grads = jnp.stack([gain_early, gain_late, bias_early, bias_late])
-        operands = (
-            normed, projected_grad, mixed, resid_low, inner_all, upward_grad, incoming_all, active,
-            vector_grads,
-        )
-        return sent_grad, operands
-
-    first, kept_first = forward(0, mine(block_input)[0])
-    second, kept_second = forward(1, first)
-    grad_second, operands_second = backward(1, mine(cotangent)[0], kept_second)
-    grad_first, operands_first = backward(0, grad_second, kept_first)
+        normed, mixed, inner, act = operands
+        return sent, (normed, projected, mixed, low, inner, up_grad, incoming_all, act, vectors)
+
+    first, kept_first, ops_first = forward(0, mine(block_input)[0])
+    second, kept_second, ops_second = forward(1, first)
+    grad_second, operands_second = backward(1, mine(cotangent)[0], kept_second, ops_second)
+    grad_first, operands_first = backward(0, grad_second, kept_first, ops_first)
 
     def swap(of_first, of_second):
         keep = jnp.where(section == 0, of_first, of_second)
@@ -612,16 +887,18 @@
 
     ga = jnp.concatenate([dot_tn(normed, projected_grad), dot_tn(mixed, resid_low)], 1)
     gb = jnp.concatenate([dot_tn(inner_all, upward_grad), dot_tn(incoming_all, active)], 1)
-    gn = vector_grads.reshape(4, 8, depth).transpose(1, 0, 2)
-    gn = jnp.pad(gn, ((0, 0), (0, 4), (0, 128 - depth)))
+    gn = vector_grads.reshape(8, 8, depth).transpose(1, 0, 2)
+    gn = jnp.pad(gn, ((0, 0), (0, 0), (0, 128 - depth)))
     out_a, out_b, out_n = reduce_grads(
         ga.astype(BF16).reshape(8, depth, -1), gb.astype(BF16).reshape(8, depth, -1), gn
     )
     out_n = out_n[:4, :depth]
+    pairs = out_a[:, width : 3 * width].reshape(depth, heads, 2, HEAD_DIM).transpose(0, 2, 1, 3)
+    out_qkv = jnp.concatenate([out_a[:, :width], pairs.reshape(depth, 2 * width)], 1)
     return (
         block_outputs[None, :, None],
         input_grads[None, :, None],
-        out_a[None, :, : 3 * width],
+        out_qkv[None],
         out_a[None, :, 3 * width :],
         out_b[None, :, :units],
         out_b[:, units:].T[None],

time: 518 us -> 392 us (0.76)
  matrix products: 80.3 us -> 7.91 us
  other arithmetic: 48 us -> 16.6 us
  local copies, waits for them, and re-layouts: 45.9 us -> 14.9 us
  Pallas kernels: 332 us -> 342 us
    dot_general x28 -> x0, matrix products: 73.6 us -> none  [the longest x8 25.9 us: dot(): return jnp.dot(first, second, preferred_element_type=F32)]
    reduce_sum x16 -> x0, other arithmetic: 15.5 us -> none  [the longest x2 3.8 us: forward(): totals = jax.nn.logsumexp(masked, axis=-1)]
    pallas_call x18 -> x6, Pallas kernels: 332 us -> 342 us  [call_remote(): pl.pallas_call(body, out_shape=out_shape, in_specs=in_specs, out_specs=ou...]
    concatenate x5 -> x0, other arithmetic: 6.96 us -> none  [the longest x1 2.78 us: per_device(): jnp.concatenate([dot_tn(inner_all, upward_grad), dot_tn(incoming_all, act...]
    convert_element_type x7 -> x1, other arithmetic: 7.85 us -> 1.1 us  [per_device(): full[:, :, 4 * width + 2 * units:4 * width + 2 * units + 8]]
    reshape x24 -> x5, local copies, waits for them, and re-layouts: 6.51 us -> 0.42 us  [the longest x1 0.17 us: per_device(): pairs.reshape(depth, 2 * width)]
    slice x19 -> x5, local copies, waits for them, and re-layouts: 7.74 us -> 1.66 us  [the longest x2 1.2 us: per_device(): w_qkv[0][:, width:].reshape(depth, 2, heads, HEAD_DIM).transpose(0, 2, 1, 3)]
    convert_element_type x12 -> x0, local copies, waits for them, and re-layouts: 5.61 us -> none  [the longest x2 1.9 us: backward(): mixed_grad = dot_nt(resid_low, out).astype(BF16)]
  transfers between devices with their start and end apart: 11 -> 11, of which waited for: 0 -> 1; matrix products, arithmetic and copies ran while one was open for 21% -> 5% of each run, Pallas kernels for 19% -> 0%
where the time goes in v2:
time: 392 us; the launch traced here: 387 us
  Pallas kernels  342 us (87%)
  other arithmetic  16.6 us (4%)
  local copies, waits for them, and re-layouts  14.9 us (4%)
  matrix products  7.91 us (2%)
    pallas_call x6, Pallas kernels, call_remote(): pl.pallas_call(body, out_shape=out_shape, in_specs=in_specs, out_specs=ou...  342 us
    dot_general x4, matrix products, dot_tn(): lax.dot_general(first, second, (((0,), (0,)), ((), ())), preferred_elemen...  7.91 us
  transfers between devices with their start and end apart: 11, of which 1 were waited for; matrix products, arithmetic and copies ran while one was open for 5% of the time, Pallas kernels for 0%

profile of v2, /device:TPU:0, one launch (start us, length us, event | category | flops | bytes accessed | tf_op | source)
XLA Modules:
  0.0 387.0 jit_solution(16814823407722717965)
XLA Ops:
  0.7 0.7 constant_dynamic-slice_fusion
  1.4 0.7 fusion.29.segk_ref
  2.1 1.0 slice.59
  3.1 0.9 slice_dynamic-update-slice_fusion
  4.3 0.2 copy.44
  4.9 0.2 copy-done.11
  5.3 0.2 copy-done.10
  5.6 1.1 copy-done.4
  6.6 69.2 %shard_map.160 = bf16[2,8,96,6272]{3,2,1,0:T(8,128)(2,1)} custom-call(bf16[96,6272]{1,0:T(8,128)(2,1)} %copy-done.4), custom_call_target="tpu_custom_call" | custom-call | tf_op jit(solution)/shard_map/pallas_call | solution.py:53
  75.9 1.1 convert_bitcast_fusion
  77.3 45.5 %shard_map.161 = (bf16[128,768]{1,0:T(8,128)(2,1)S(1)}, bf16[128,768]{1,0:T(8,128)(2,1)S(1)}, bf16[4,128,256]{2,1,0:T(8,128)(2,1)S(1)}, bf16[8,128,384]{2,1,0:T(...) custom-call(bf16[128,768]{1,0:T(8,128)(2,1)S(1)} %dynamic-slice_bitc, ...), custom_call_target="tpu_custom_call" | custom-call | tf_op jit(solution)/shard_map/pallas_call | solution.py:53
  122.8 1.1 copy-done.2
  124.0 39.2 %shard_map.162 = (bf16[128,768]{1,0:T(8,128)(2,1)S(1)}, bf16[128,768]{1,0:T(8,128)(2,1)S(1)}, bf16[4,128,256]{2,1,0:T(8,128)(2,1)S(1)}, bf16[8,128,384]{2,1,0:T(...) custom-call(bf16[128,768]{1,0:T(8,128)(2,1)S(1)} %get-tuple-element., ...), custom_call_target="tpu_custom_call" | custom-call | tf_op jit(solution)/shard_map/pallas_call | solution.py:53
  163.2 1.2 copy-done.3
  164.3 44.1 %shard_map.163 = (bf16[128,768]{1,0:T(8,128)(2,1)S(1)}, bf16[128,2304]{1,0:T(8,128)(2,1)S(1)}, bf16[128,768]{1,0:T(8,128)(2,1)S(1)}, bf16[256,768]{1,0:T(8,128)(...) custom-call(bf16[128,768]{1,0:T(8,128)(2,1)S(1)} %dynamic-slice_bitcast_fusion.dy_ref, ...), custom_call_target="tpu_custom_call" | custom-call | tf_op jit(solution)/shard_map/pallas_call | solution.py:53
  208.4 41.0 %shard_map.164 = (bf16[128,768]{1,0:T(8,128)(2,1)S(1)}, bf16[128,2304]{1,0:T(8,128)(2,1)S(1)}, bf16[128,768]{1,0:T(8,128)(2,1)S(1)}, bf16[256,768]{1,0:T(8,128)(...) custom-call(bf16[128,768]{1,0:T(8,128)(2,1)S(1)} %get-tuple-element.51.dy_ref, ...), custom_call_target="tpu_custom_call" | custom-call | tf_op jit(solution)/shard_map/pallas_call | solution.py:53
  249.7 0.6 collective-permute-start.7
  250.3 0.9 broadcast_select_fusion.5
  251.2 0.7 broadcast_select_fusion.11
  251.9 0.5 collective-permute-start.5
  252.4 0.8 broadcast_select_fusion.13
  253.2 0.7 select_bitcast_fusion
  253.9 0.9 broadcast_select_fusion.9
  254.8 0.8 broadcast_select_fusion.7
  255.6 1.3 broadcast_select_fusion.1
  256.9 0.7 broadcast_select_fusion.15
  257.6 0.7 select_bitcast_fusion.1
  258.3 0.5 collective-permute-start.1
  258.9 0.6 copy-done.15
  259.6 0.6 collective-permute-done.1
  260.2 0.4 collective-permute-start.9
  260.5 1.8 maximum_select_fusion.1
  262.5 0.4 collective-permute-start.2
  262.9 1.8 maximum_select_fusion
  264.7 1.6 convolution_convert_fusion.3
  266.4 0.5 collective-permute-start.8
  266.8 2.2 convolution_convert_fusion
  269.1 2.6 convolution_convert_fusion.2
  271.8 1.4 convolution_convert_fusion.1
  273.2 4.2 %pad_maximum_fusion = (bf16[8,96,3072]{2,1,0:T(8,128)(2,1)}, bf16[8,96,3072]{2,1,0:T(8,128)(2,1)}) fusion(bf16[8,96,768]{2,1,0:T(8,128)(2,1)S(1)} %bitcast.73, bf16[8,96,2304]{2,1,0:T(8,128)(2,1)S(1)} %bitcast.66, bf16[8,96,1536]{2,1,0:T(8,128)(2,1)S(1)} %bitcast.70, bf16[8,96,1536]{2,1,0:T(8,128)(2,1)S(1)} %bitcast.69), kind=kLoop, calls=%fused_computation.1 | loop fusion | flops 18874368 | bytes 18874368 | tf_op jit(solution)/shard_map/concatenate | solution.py:888
  277.4 103.4 %shard_map.165 = (f32[96,3072]{1,0:T(8,128)S(1)}, f32[96,3072]{1,0:T(8,128)S(1)}, f32[8,128]{1,0:T(8,128)S(1)}) custom-call(bf16[8,96,3072]{2,1,0:T(8,128)(2,1)} %get-tuple-element.125.ga, bf16[8,96,3072]{2,1,0:T(8,128)(2,1)} %get-tuple-element.126.gb, f32[8,8,128]{2,1,0:T(8,128)S(1)} %pad.9.gn), custom_call_target="tpu_custom_call" | custom-call | tf_op jit(solution)/shard_map/pallas_call | solution.py:53
  380.9 0.9 slice_bitcast_fusion.4
  381.7 0.5 fusion.28
  382.3 0.6 slice_bitcast_fusion.5
  382.8 0.3 copy.57
  383.2 0.9 copy-done.5
  384.3 1.3 copy.60
  385.6 1.1 slice_bitcast_fusion
  (68 shorter events, 2.1 us)
Async XLA Ops:
  0.6 3.6 copy-start
  3.1 1.7 copy-start.13
  3.1 1.7 copy-start.14
  4.2 0.9 copy-start.11
  4.3 1.0 copy-start.9
  4.5 1.0 copy-start.10
  5.6 1.1 copy-start.4
  75.9 1.4 copy-start.12
  122.8 1.2 copy-start.2
  163.1 1.2 copy-start.3
  249.5 8.8 %collective-permute-start.10 = (f32[8,768]{1,0:T(8,128)S(1)}, f32[8,768]{1,0:T(8,128)S(1)}, u32[]{:S(2)}, u32[]{:S(2)}) collective-permute-start(f32[8,768]{1,0:T(8,128)S(1)} %broadcast_select_fusion.18), channel_id=1, source_target_pairs={{0,64},{64,0},{1,65},{65,1},{2,66},{66,2},{3,67},{67,3},{4,68},{68... | collective-permute-start | bytes 73736 | tf_op jit(solution)/shard_map/ppermute | solution.py:870
  249.7 19.4 %collective-permute-start.7 = (bf16[256,1536]{1,0:T(8,128)(2,1)S(1)}, bf16[256,1536]{1,0:T(8,128)(2,1)}, u32[]{:S(2)}, u32[]{:S(2)}) collective-permute-start(bf16[256,1536]{1,0:T(8,128)(2,1)S(1)} %get-tuple-element.98), channel_id=1, source_target_pairs={{0,64},{64,0},{1,65},{65,1},{2,66},{66,2},{3,67},{67,3},{4,68},{68... | collective-permute-start | bytes 2359304 | tf_op jit(solution)/shard_map/ppermute | solution.py:870
  251.2 15.7 %collective-permute-start.3 = (bf16[128,2304]{1,0:T(8,128)(2,1)}, bf16[128,2304]{1,0:T(8,128)(2,1)}, u32[]{:S(2)}, u32[]{:S(2)}) collective-permute-start(bf16[128,2304]{1,0:T(8,128)(2,1)} %get-tuple-element.106), channel_id=1, source_target_pairs={{0,64},{64,0},{1,65},{65,1},{2,66},{66,2},{3,67},{67,3},{4,68},{68... | collective-permute-start | bytes 1769480 | tf_op jit(solution)/shard_map/ppermute | solution.py:870
  251.9 6.9 %collective-permute-start.5 = (bf16[128,768]{1,0:T(8,128)(2,1)S(1)}, bf16[128,768]{1,0:T(8,128)(2,1)S(1)}, u32[]{:S(2)}, u32[]{:S(2)}) collective-permute-start(bf16[128,768]{1,0:T(8,128)(2,1)S(1)} %get-tuple-element.116), channel_id=1, source_target_pairs={{0,64},{64,0},{1,65},{65,1},{2,66},{66,2},{3,67},{67,3},{4,68},{68... | collective-permute-start | bytes 589832 | tf_op jit(solution)/shard_map/ppermute | solution.py:870
  253.1 9.2 %collective-permute-start.4 = (bf16[128,768]{1,0:T(8,128)(2,1)}, bf16[128,768]{1,0:T(8,128)(2,1)}, u32[]{:S(2)}, u32[]{:S(2)}) collective-permute-start(bf16[128,768]{1,0:T(8,128)(2,1)} %get-tuple-element.118), channel_id=1, source_target_pairs={{0,64},{64,0},{1,65},{65,1},{2,66},{66,2},{3,67},{67,3},{4,68},{68... | collective-permute-start | bytes 589832 | tf_op jit(solution)/shard_map/ppermute | solution.py:870
  258.3 1.9 collective-permute-start.1
  258.8 0.7 copy-start.15
  258.8 3.8 collective-permute-start
  259.5 5.2 %copy-start.16 = (bf16[128,768]{1,0:T(8,128)(2,1)S(1)}, bf16[128,768]{1,0:T(8,128)(2,1)}, u32[]{:S(2)}) copy-start(bf16[128,768]{1,0:T(8,128)(2,1)} %copy-done.15) | copy-start | bytes 589828
  260.2 11.6 %collective-permute-start.9 = (bf16[256,1536]{1,0:T(8,128)(2,1)}, bf16[256,1536]{1,0:T(8,128)(2,1)S(1)}, u32[]{:S(2)}, u32[]{:S(2)}) collective-permute-start(bf16[256,1536]{1,0:T(8,128)(2,1)} %get-tuple-element.100), channel_id=1, source_target_pairs={{0,64},{64,0},{1,65},{65,1},{2,66},{66,2},{3,67},{67,3},{4,68},{68... | collective-permute-start | bytes 2359304 | tf_op jit(solution)/shard_map/ppermute | solution.py:870
  262.4 4.0 %copy-start.8 = (bf16[256,768]{1,0:T(8,128)(2,1)S(1)}, bf16[256,768]{1,0:T(8,128)(2,1)}, u32[]{:S(2)}) copy-start(bf16[256,768]{1,0:T(8,128)(2,1)} %get-tuple-element.110) | copy-start | bytes 1179652
  262.4 6.7 %collective-permute-start.6 = (bf16[256,768]{1,0:T(8,128)(2,1)}, bf16[256,768]{1,0:T(8,128)(2,1)S(1)}, u32[]{:S(2)}, u32[]{:S(2)}) collective-permute-start(bf16[256,768]{1,0:T(8,128)(2,1)} %get-tuple-element.108), channel_id=1, source_target_pairs={{0,64},{64,0},{1,65},{65,1},{2,66},{66,2},{3,67},{67,3},{4,68},{68... | collective-permute-start | bytes 1179656 | tf_op jit(solution)/shard_map/ppermute | solution.py:870
  262.5 3.8 collective-permute-start.2
  266.4 5.4 %collective-permute-start.8 = (bf16[256,768]{1,0:T(8,128)(2,1)S(1)}, bf16[256,768]{1,0:T(8,128)(2,1)S(1)}, u32[]{:S(2)}, u32[]{:S(2)}) collective-permute-start(bf16[256,768]{1,0:T(8,128)(2,1)S(1)} %copy-done.8), channel_id=1, source_target_pairs={{0,64},{64,0},{1,65},{65,1},{2,66},{66,2},{3,67},{67,3},{4,68},{68... | collective-permute-start | bytes 1179656 | tf_op jit(solution)/shard_map/ppermute | solution.py:870
  266.8 2.3 copy-start.7
  269.1 2.7 copy-start.6
  383.1 1.0 copy-start.5
  384.3 2.4 copy-start.1
